TPU v7x, 256 devices: a whole 4x4x8 slice. The times are simulated.
256 devices in a mesh: ctx: 64 (over x, y, z_hi, core), ch: 4 (over z_lo).
Axes of the slice: x: 4, y: 4, z: 8 (z_hi: 2, z_lo: 4; z = z_hi * 4 + z_lo), core: 2. Of those that a mesh axis runs over, the one named last changes fastest.
Arguments:
- out_gate: bfloat16 [16384, 4096], P('ctx', 'ch'), may hold values from -6 to 6
- in_gate: bfloat16 [16384, 4096], P('ctx', 'ch'), may hold values from -6 to 6
- values: bfloat16 [16384, 4096], P('ctx', 'ch'), may hold values from -6 to 6
- filter_taps: bfloat16 [16384, 4096], P('ctx', 'ch'), may hold values from -0.046875 to 0.046875
- out_grad: bfloat16 [16384, 4096], P('ctx'), may hold values from -16 to 16
- out_weight: bfloat16 [4096, 4096], P('ch', 'ctx'), may hold values from -0.09375 to 0.09375
Outputs:
- out_gate_grad: bfloat16 [16384, 4096], P('ctx', 'ch')
- in_gate_grad: bfloat16 [16384, 4096], P('ctx', 'ch')
- values_grad: bfloat16 [16384, 4096], P('ctx', 'ch')
- taps_grad: float32 [16384, 4096], P('ctx', 'ch')
- weight_grad: float32 [4096, 4096], P('ch', 'ctx')
All inputs are finite; a program needn't handle non-finite values.
Results may differ from a plain program's by a relative error of at most 0.0065.
Values may be sent and summed in bfloat16 or wider, within the bound.
A program may use at most 128 MiB of HBM per device.

v0:
```python
import math

import jax
import jax.numpy as jnp
from jax import lax
from jax.sharding import PartitionSpec as P

highest = lax.Precision.HIGHEST


def contract(form, left, right):
    return jnp.einsum(form, left, right, precision=highest, preferred_element_type=jnp.float32)


def phase_table(row_count, col_count, period):
    rows = jnp.arange(row_count, dtype=jnp.int32)[:, None]
    cols = jnp.arange(col_count, dtype=jnp.int32)[None, :]
    turns = (rows * cols % period).astype(jnp.float32) * (2.0 * math.pi / period)
    return (jnp.cos(turns), jnp.sin(turns))


def spectrum(signal, blocks_a, blocks_b):
    chans = signal.shape[0]
    half = blocks_a // 2
    grid = signal.reshape(chans, half, blocks_b)
    cos_a, sin_a = phase_table(blocks_a, half, blocks_a)
    table_a = jnp.stack([cos_a, -sin_a])
    first = contract("pkn,cnm->cpkm", table_a, grid)
    first_re = first[:, 0]
    first_im = first[:, 1]
    cos_t, sin_t = phase_table(blocks_a, blocks_b, blocks_a * blocks_b)
    turned = jnp.stack(
        [first_re * cos_t + first_im * sin_t, first_im * cos_t - first_re * sin_t], axis=1
    )
    cos_b, sin_b = phase_table(blocks_b, blocks_b, blocks_b)
    table_b = jnp.stack([jnp.stack([cos_b, -sin_b]), jnp.stack([sin_b, cos_b])])
    spec = contract("cpkm,pqmj->cqkj", turned, table_b)
    return (spec[:, 0], spec[:, 1])


def signal_of(spec_re, spec_im, real_only):
    chans, blocks_a, blocks_b = spec_re.shape
    half = blocks_a // 2
    scale = 1.0 / (blocks_a * blocks_b)
    cos_b, sin_b = phase_table(blocks_b, blocks_b, blocks_b)
    table_b = jnp.stack([jnp.stack([cos_b, sin_b]), jnp.stack([-sin_b, cos_b])])
    first = contract("cpkj,pqjm->cqkm", jnp.stack([spec_re, spec_im], axis=1), table_b)
    first_re = first[:, 0]
    first_im = first[:, 1]
    cos_t, sin_t = phase_table(blocks_a, blocks_b, blocks_a * blocks_b)
    turned = jnp.stack(
        [first_re * cos_t - first_im * sin_t, first_re * sin_t + first_im * cos_t], axis=1
    )
    cos_a, sin_a = phase_table(blocks_a, half, blocks_a)
    table_a = jnp.stack([jnp.stack([cos_a, sin_a]), jnp.stack([-sin_a, cos_a])])
    if real_only:
        table_a = table_a[:, :1]
    outs = contract("pqkn,cpkm->cqnm", table_a, turned) * scale
    out_re = outs[:, 0].reshape(chans, half * blocks_b)
    if real_only:
        return out_re
    return (out_re, outs[:, 1].reshape(chans, half * blocks_b))


def convolve(gated, grad_conv, taps):
    length = gated.shape[1]
    blocks_b = 128
    blocks_a = 2 * length // blocks_b
    gated_re, gated_im = spectrum(gated.astype(jnp.float32), blocks_a, blocks_b)
    grad_re, grad_im = spectrum(grad_conv.astype(jnp.float32), blocks_a, blocks_b)
    taps_re, taps_im = spectrum(taps.astype(jnp.float32), blocks_a, blocks_b)
    fwd_re = taps_re * gated_re - taps_im * gated_im
    fwd_im = taps_re * gated_im + taps_im * gated_re
    back_re = taps_re * grad_re + taps_im * grad_im
    back_im = taps_re * grad_im - taps_im * grad_re
    conv, grad_gated = signal_of(fwd_re - back_im, fwd_im + back_re, False)
    corr_re = gated_re * grad_re + gated_im * grad_im
    corr_im = gated_re * grad_im - gated_im * grad_re
    taps_grad = signal_of(corr_re, corr_im, True)
    return (conv.astype(jnp.bfloat16), grad_gated.astype(jnp.bfloat16), taps_grad)


def product(left, right):
    return (left.astype(jnp.float32) * right.astype(jnp.float32)).astype(jnp.bfloat16)


def on_device(out_gate, in_gate, values, filter_taps, out_grad, out_weight):
    gathered = lax.all_gather(out_weight, "ctx", axis=1, tiled=True)
    grad_y = lax.dot_general(
        out_grad, gathered, (((1,), (1,)), ((), ())), preferred_element_type=jnp.float32
    ).astype(jnp.bfloat16)
    taps_grad = None
    gate_c, input_c, values_c, grad_c, taps_c = (
        lax.all_to_all(out_gate.T, "ctx", split_axis=0, concat_axis=1, tiled=True),
        lax.all_to_all(in_gate.T, "ctx", split_axis=0, concat_axis=1, tiled=True),
        lax.all_to_all(values.T, "ctx", split_axis=0, concat_axis=1, tiled=True),
        lax.all_to_all(grad_y.T, "ctx", split_axis=0, concat_axis=1, tiled=True),
        lax.all_to_all(filter_taps.T, "ctx", split_axis=0, concat_axis=1, tiled=True),
    )
    gated_c = product(input_c, values_c)
    conv_grad_c = product(grad_c, gate_c)
    conv_c, grad_gated_c, taps_grad_c = convolve(gated_c, conv_grad_c, taps_c)
    sending = (
        product(grad_c, conv_c),
        product(grad_gated_c, values_c),
        product(grad_gated_c, input_c),
        product(gate_c, conv_c),
    )
    back = (
        lax.all_to_all(sending[0], "ctx", split_axis=1, concat_axis=0, tiled=True),
        lax.all_to_all(sending[1], "ctx", split_axis=1, concat_axis=0, tiled=True),
        lax.all_to_all(sending[2], "ctx", split_axis=1, concat_axis=0, tiled=True),
        lax.all_to_all(sending[3], "ctx", split_axis=1, concat_axis=0, tiled=True),
    )
    out_gate_grad = back[0].T
    in_gate_grad = back[1].T
    values_grad = back[2].T
    mixed = back[3].T
    taps_grad = (
        lax.all_to_all(
            taps_grad_c.astype(jnp.bfloat16), "ctx", split_axis=1, concat_axis=0, tiled=True
        )
        .astype(taps_grad_c.dtype)
        .T
    )
    share = lax.psum_scatter(
        lax.dot_general(
            out_grad, mixed, (((0,), (0,)), ((), ())), preferred_element_type=jnp.float32
        ),
        "ctx",
        scatter_dimension=0,
        tiled=True,
    )
    return (out_gate_grad, in_gate_grad, values_grad, taps_grad, share.T)


def solution(mesh):
    return jax.shard_map(
        on_device,
        mesh=mesh,
        in_specs=(
            P("ctx", "ch"),
            P("ctx", "ch"),
            P("ctx", "ch"),
            P("ctx", "ch"),
            P("ctx", None),
            P("ch", "ctx"),
        ),
        out_specs=(P("ctx", "ch"), P("ctx", "ch"), P("ctx", "ch"), P("ctx", "ch"), P("ch", "ctx")),
        check_vma=False,
    )
```

profile of v0, /device:TPU:32, one launch (start us, length us, event | category | flops | bytes accessed | tf_op | source)
XLA Modules:
  0.0 846.1 jit_solution(12488067540155358509)
XLA Ops:
  7.9 2.1 copy.77
  10.0 13.7 %all-to-all-start.4 = ((bf16[64,16,256]{2,1,0:T(8,128)(2,1)}), bf16[64,16,256]{2,1,0:T(8,128)(2,1)S(1)}, u32[]{:S(2)}, u32[]{:S(2)}) async-start(bf16[64,16,256]{2,1,0:T(8,128)(2,1)} %bitcast.36), calls=%async_computation.4 | async-start | bytes 1048576 | tf_op jit(solution)/shard_map/all_to_all | solution.py:94
  24.7 23.2 %all-to-all-done.4 = bf16[64,16,256]{2,1,0:T(8,128)(2,1)S(1)} async-done(((bf16[64,16,256]{2,1,0:T(8,128)(2,1)}), bf16[64,16,256]{2,1,0:T(8,128)(2,1)S(1)}, u32[]{:S(2)}, u32[]{:S(2)}) %all-to-all-start.4) | async-done | bytes 524320 | tf_op jit(solution)/shard_map/all_to_all | solution.py:94
  48.6 4.6 all-to-all-start.2
  53.3 2.0 copy.72
  55.3 23.6 %all-to-all-done.2 = bf16[64,16,256]{2,1,0:T(8,128)(2,1)S(1)} async-done(((bf16[64,16,256]{2,1,0:T(8,128)(2,1)}), bf16[64,16,256]{2,1,0:T(8,128)(2,1)S(1)}, u32[]{:S(2)}, u32[]{:S(2)}) %all-to-all-start.2) | async-done | bytes 524320 | tf_op jit(solution)/shard_map/all_to_all | solution.py:95
  78.9 4.6 all-to-all-start.3
  83.6 2.0 copy.68
  88.2 14.2 %all-to-all-done.3 = bf16[64,16,256]{2,1,0:T(8,128)(2,1)S(1)} async-done(((bf16[64,16,256]{2,1,0:T(8,128)(2,1)}), bf16[64,16,256]{2,1,0:T(8,128)(2,1)S(1)}, u32[]{:S(2)}, u32[]{:S(2)}) %all-to-all-start.3) | async-done | bytes 524320 | tf_op jit(solution)/shard_map/all_to_all | solution.py:96
  102.4 5.5 all-to-all-start.1
  111.6 11.6 %all-gather.2.cloned.1.call-done = bf16[1024,4096]{0,1:T(8,128)(2,1)} async-done(((bf16[1024,64]{0,1:T(8,128)(2,1)}), bf16[1024,4096]{0,1:T(8,128)(2,1)}) %all-gather.2.cloned.1.call-update) | async-done | bytes 8388624 | tf_op jit(solution)/shard_map/all_gather | solution.py:88
  123.2 6.6 convolution_convert_fusion
  131.5 9.9 %all-to-all-start = ((bf16[64,16,256]{2,1,0:T(8,128)(2,1)}), bf16[64,16,256]{2,1,0:T(8,128)(2,1)}, u32[]{:S(2)}, u32[]{:S(2)}) async-start(bf16[64,16,256]{2,1,0:T(8,128)(2,1)} %bitcast.220), calls=%async_computation | async-start | bytes 1048576 | tf_op jit(solution)/shard_map/all_to_all | solution.py:97
  144.0 2.0 convert_element_type.271
  149.9 4.9 convolution_bitcast_fusion.3
  154.9 3.8 convolution_bitcast_fusion.2
  162.9 3.0 convolution_bitcast_fusion.1
  166.0 3.4 multiply_add_fusion.4
  169.4 4.1 fusion.22
  173.6 4.2 fusion.25
  177.7 4.2 fusion.19
  183.3 2.8 subtract_subtract_fusion
  186.1 7.1 fusion.31
  193.2 7.2 fusion.28
  200.4 3.3 multiply_subtract_fusion
  203.7 7.1 fusion.37
  212.4 2.6 copy.87
  214.9 2.5 reshape.270
  217.4 3.1 fusion.58
  220.6 29.2 %all_to_all.142 = bf16[16,64,256]{2,0,1:T(8,128)(2,1)S(1)} all-to-all(bf16[16,64,256]{2,0,1:T(8,128)(2,1)S(1)} %get-tuple-element.34), channel_id=1, replica_groups=mesh['ctx'=64,'ch'=4] {'ctx'}, dimensions={1} | all-to-all | bytes 1048576 | tf_op jit(solution)/shard_map/all_to_all | solution.py:113
  249.8 8.1 convolution_bitcast_fusion
  257.9 17.4 %copy.137 = f32[4096,1024]{1,0:T(8,128)} copy(f32[4096,1024]{0,1:T(8,128)} %convolution_bitcast_fusion) | data formatting | bytes 33554432
  275.3 9.7 %fusion.49 = bf16[16,1,128,128]{2,3,0,1:T(8,128)(2,1)} fusion(f32[16,1,256,128]{3,2,0,1:T(8,128)} %get-tuple-element.25, f32[16,1,256,128]{3,2,0,1:T(8,128)} %get-tuple-element.24, f32[1,2,256,128]{3,2,1,0:T(8,128)S(1)} %copy-done.11, f32[1,2,256,128]{3,2,1,0:T(8,128)} %get-tuple-element.47), kind=kOutput, calls=%fused_computation.61 | convolution fusion | flops 1612251136 | bytes 5242880 | tf_op jit(solution)/shard_map/pqkn,cpkm->cqnm/dot_general | solution.py:12
  285.0 2.0 copy.96
  289.1 2.1 copy.97
  291.2 5.7 all-to-all-start.8
  297.0 2.6 copy.89
  299.5 2.5 reshape.271
  302.0 2.8 fusion.53
  304.8 8.8 %all-to-all-done.8 = bf16[16,64,256]{2,0,1:T(8,128)(2,1)} async-done(((bf16[16,64,256]{2,0,1:T(8,128)(2,1)}), bf16[16,64,256]{2,0,1:T(8,128)(2,1)}, u32[]{:S(2)}, u32[]{:S(2)}) %all-to-all-start.8) | async-done | bytes 524320 | tf_op jit(solution)/shard_map/all_to_all | solution.py:120
  313.6 37.6 %all_to_all.143 = bf16[16,64,256]{2,0,1:T(8,128)(2,1)} all-to-all(bf16[16,64,256]{2,0,1:T(8,128)(2,1)} %get-tuple-element.36), channel_id=1, replica_groups=mesh['ctx'=64,'ch'=4] {'ctx'}, dimensions={1} | all-to-all | bytes 1048576 | tf_op jit(solution)/shard_map/all_to_all | solution.py:112
  351.2 39.0 %all_to_all.144 = bf16[16,64,256]{2,0,1:T(8,128)(2,1)} all-to-all(bf16[16,64,256]{2,0,1:T(8,128)(2,1)} %get-tuple-element.37), channel_id=1, replica_groups=mesh['ctx'=64,'ch'=4] {'ctx'}, dimensions={1} | all-to-all | bytes 1048576 | tf_op jit(solution)/shard_map/all_to_all | solution.py:111
  390.2 8.5 %all-to-all-start.5 = ((bf16[16,64,256]{2,0,1:T(8,128)(2,1)}), bf16[16,64,256]{2,0,1:T(8,128)(2,1)}, u32[]{:S(2)}, u32[]{:S(2)}) async-start(bf16[16,64,256]{2,0,1:T(8,128)(2,1)} %get-tuple-element.35), calls=%async_computation.5 | async-start | bytes 1048576 | tf_op jit(solution)/shard_map/all_to_all | solution.py:110
  401.2 2.0 copy.101
  403.2 2.0 copy.100
  405.3 22.1 %all-to-all-done.5 = bf16[16,64,256]{2,0,1:T(8,128)(2,1)} async-done(((bf16[16,64,256]{2,0,1:T(8,128)(2,1)}), bf16[16,64,256]{2,0,1:T(8,128)(2,1)}, u32[]{:S(2)}, u32[]{:S(2)}) %all-to-all-start.5) | async-done | bytes 524320 | tf_op jit(solution)/shard_map/all_to_all | solution.py:110
  427.4 2.0 copy.99
  429.5 409.3 %reduce-scatter.4.cloned.1.call-done = f32[64,1024]{1,0:T(8,128)} async-done(((f32[4096,1024]{1,0:T(8,128)}), f32[64,1024]{1,0:T(8,128)}) %reduce-scatter.4.cloned.1.call-update) | async-done | bytes 262160
  (54 shorter events, 28.9 us)
Async XLA Ops:
  7.2 116.0 %copy-start = (bf16[256,4096]{1,0:T(8,128)(2,1)S(1)}, bf16[256,4096]{1,0:T(8,128)(2,1)}, u32[]{:S(2)}) copy-start(bf16[256,4096]{1,0:T(8,128)(2,1)} %param.10) | copy-start | bytes 6291460
  7.2 16.5 %copy-start.13 = (bf16[256,1024]{1,0:T(8,128)(2,1)S(1)}, bf16[256,1024]{1,0:T(8,128)(2,1)}, u32[]{:S(2)}) copy-start(bf16[256,1024]{1,0:T(8,128)(2,1)} %param.7) | copy-start | bytes 1572868
  7.2 116.0 %all-gather.2.cloned.1.call-start = ((), (), s32[]{:S(2)}) async-start(), calls=%async_computation.11 | async-start | bytes 8519680 | tf_op jit(solution)/shard_map/all_gather | solution.py:88
  10.0 37.9 %all-to-all-start.4 = ((bf16[64,16,256]{2,1,0:T(8,128)(2,1)}), bf16[64,16,256]{2,1,0:T(8,128)(2,1)S(1)}, u32[]{:S(2)}, u32[]{:S(2)}) async-start(bf16[64,16,256]{2,1,0:T(8,128)(2,1)} %bitcast.36), calls=%async_computation.4 | async-start | bytes 1048576 | tf_op jit(solution)/shard_map/all_to_all | solution.py:94
  47.9 0.8 copy-start.3
  48.6 30.3 %all-to-all-start.2 = ((bf16[64,16,256]{2,1,0:T(8,128)(2,1)}), bf16[64,16,256]{2,1,0:T(8,128)(2,1)S(1)}, u32[]{:S(2)}, u32[]{:S(2)}) async-start(bf16[64,16,256]{2,1,0:T(8,128)(2,1)} %bitcast.22), calls=%async_computation.2 | async-start | bytes 1048576 | tf_op jit(solution)/shard_map/all_to_all | solution.py:95
  78.9 23.4 %all-to-all-start.3 = ((bf16[64,16,256]{2,1,0:T(8,128)(2,1)}), bf16[64,16,256]{2,1,0:T(8,128)(2,1)S(1)}, u32[]{:S(2)}, u32[]{:S(2)}) async-start(bf16[64,16,256]{2,1,0:T(8,128)(2,1)} %bitcast.217), calls=%async_computation.3 | async-start | bytes 1048576 | tf_op jit(solution)/shard_map/all_to_all | solution.py:96
  102.4 29.1 %all-to-all-start.1 = ((bf16[64,16,256]{2,1,0:T(8,128)(2,1)}), bf16[64,16,256]{2,1,0:T(8,128)(2,1)}, u32[]{:S(2)}, u32[]{:S(2)}) async-start(bf16[64,16,256]{2,1,0:T(8,128)(2,1)} %bitcast.216), calls=%async_computation.1 | async-start | bytes 1048576 | tf_op jit(solution)/shard_map/all_to_all | solution.py:98
  131.5 27.2 %all-to-all-start = ((bf16[64,16,256]{2,1,0:T(8,128)(2,1)}), bf16[64,16,256]{2,1,0:T(8,128)(2,1)}, u32[]{:S(2)}, u32[]{:S(2)}) async-start(bf16[64,16,256]{2,1,0:T(8,128)(2,1)} %bitcast.220), calls=%async_computation | async-start | bytes 1048576 | tf_op jit(solution)/shard_map/all_to_all | solution.py:97
  141.4 697.4 %reduce-scatter.4.cloned.1.call-start = ((), (), s32[]{:S(2)}) async-start(), calls=%async_computation.12 | async-start | bytes 17039360
  149.9 4.9 copy-start.5
  162.9 3.0 copy-start.1
  162.9 3.0 copy-start.6
  162.9 3.0 copy-start.7
  166.0 3.4 copy-start.4
  183.2 2.8 copy-start.9
  183.2 2.8 copy-start.10
  186.1 7.1 copy-start.2
  193.2 7.3 copy-start.8
  200.4 3.3 copy-start.11
  200.4 3.3 copy-start.12
  291.2 22.4 %all-to-all-start.8 = ((bf16[16,64,256]{2,0,1:T(8,128)(2,1)}), bf16[16,64,256]{2,0,1:T(8,128)(2,1)}, u32[]{:S(2)}, u32[]{:S(2)}) async-start(bf16[16,64,256]{2,0,1:T(8,128)(2,1)} %copy.97), calls=%async_computation.8 | async-start | bytes 1048576 | tf_op jit(solution)/shard_map/all_to_all | solution.py:120
  390.2 37.2 %all-to-all-start.5 = ((bf16[16,64,256]{2,0,1:T(8,128)(2,1)}), bf16[16,64,256]{2,0,1:T(8,128)(2,1)}, u32[]{:S(2)}, u32[]{:S(2)}) async-start(bf16[16,64,256]{2,0,1:T(8,128)(2,1)} %get-tuple-element.35), calls=%async_computation.5 | async-start | bytes 1048576 | tf_op jit(solution)/shard_map/all_to_all | solution.py:110
Sparse Core Ops, SparseCore 0:
  11.5 111.6 all-gather.1
  275.5 563.2 reduce-scatter.3
where the time goes:
time: 855 us; the launch traced here: 846 us
  waiting for transfers between devices  515 us (60%)
  blocking collectives  106 us (12%)
  matrix products  70 us (8%)
  local copies, waits for them, and re-layouts  59.1 us (7%)
  starting transfers between devices  52.8 us (6%)
  other arithmetic  28.6 us (3%)
  between operations  14.8 us (2%)
    unnamed x3, waiting for transfers between devices  410 us
    dot_general x10, matrix products, contract(): jnp.einsum(form, left, right, precision=highest, preferred_element_type=j...  55.3 us
    all_to_all x1, blocking collectives, on_device(): lax.all_to_all(sending[1], 'ctx', split_axis=1, concat_axis=0, tiled=True)  39 us
    all_to_all x1, blocking collectives, on_device(): lax.all_to_all(sending[2], 'ctx', split_axis=1, concat_axis=0, tiled=True)  37.6 us
    unnamed x37, local copies, waits for them, and re-layouts  32.9 us
    all_to_all x1, blocking collectives, on_device(): lax.all_to_all(sending[3], 'ctx', split_axis=1, concat_axis=0, tiled=True)  29.2 us
    all_to_all x1, waiting for transfers between devices, on_device(): lax.all_to_all(in_gate.T, 'ctx', split_axis=0, concat_axis=1, tiled=True)  23.6 us
    all_to_all x1, waiting for transfers between devices, on_device(): lax.all_to_all(out_gate.T, 'ctx', split_axis=0, concat_axis=1, tiled=True)  23.2 us
  transfers between devices with their start and end apart: 9, of which 8 were waited for; matrix products, arithmetic and copies ran while one was open for 8% of the time, Pallas kernels for 0%

commit v1 on v0

v1 whole, which is shorter than its diff:
```python
import functools

import jax
import jax.numpy as jnp
import numpy as np
from jax import lax
from jax.experimental import pallas as pl
from jax.experimental.pallas import tpu as pltpu
from jax.sharding import PartitionSpec as P

MESH = pl.DeviceIdType.MESH
F32 = jnp.float32
BF16 = jnp.bfloat16

RANKS = 64
POS = 256
CHAN = 16
WIDTH = RANKS * CHAN
MODEL = 4096
VMEM_LIMIT = 56 * 2**20


def coords():
    i = lax.axis_index("ctx")
    return i // 16, (i // 4) % 4, (i // 2) % 2, i % 2


def device(x, y, z, b):
    return (((x * 4 + y) * 2 + z) * 2 + b, lax.axis_index("ch"))


def split(x):
    hi = x.astype(BF16)
    return hi, (x - hi.astype(F32)).astype(BF16)


def tables():
    n = RANKS * POS
    k1 = np.arange(RANKS) + 0.25
    first = 2 * np.pi * k1[:, None] * np.arange(RANKS)[None, :] / RANKS
    turn = 2 * np.pi * k1[:, None] * np.arange(POS)[None, :] / n
    second = 2 * np.pi * ((np.arange(POS)[:, None] * np.arange(POS)[None, :]) % POS) / POS

    def parts(table):
        hi = table.astype(jnp.bfloat16)
        lo = (table - hi.astype(np.float64)).astype(jnp.bfloat16)
        return hi, lo

    one = np.concatenate([np.cos(first), -np.sin(first)], 0)
    one_hi, one_lo = parts(one)
    cos, sin = np.cos(second), np.sin(second)
    two_hi, two_lo = parts(np.block([[cos, -sin], [sin, cos]]))
    last = np.concatenate([np.cos(first), np.sin(first)], 0).T / n
    last_hi, last_lo = parts(last)
    return (
        np.concatenate([one_hi, one_lo], 1),
        np.cos(turn).astype(np.float32),
        (-np.sin(turn)).astype(np.float32),
        two_hi,
        two_lo,
        np.concatenate([last_hi, last_lo, last_hi], 1),
    )


def transform(rows, tabs, z_hi, z_lo, spec):
    one, cos_t, sin_t, two_hi, two_lo, _ = tabs
    for c in range(CHAN):
        x = jnp.concatenate([rows[u, pl.ds(c, RANKS, stride=CHAN), :] for u in range(2)], 1).astype(BF16)
        a = jnp.dot(one[...], jnp.concatenate([x, x], 0), preferred_element_type=F32)
        turn_in(a[:RANKS], a[RANKS:], cos_t, sin_t, z_hi, z_lo, c)
    second(z_hi, z_lo, two_hi, two_lo, spec)


def turn_in(re, im, cos_t, sin_t, z_hi, z_lo, c):
    at = slice(c * RANKS, (c + 1) * RANKS)
    z_hi[at, :POS], z_lo[at, :POS] = split(re * cos_t[...] - im * sin_t[...])
    z_hi[at, POS:], z_lo[at, POS:] = split(re * sin_t[...] + im * cos_t[...])


def second(z_hi, z_lo, two_hi, two_lo, spec):
    def block(i, carry):
        at = pl.ds(pl.multiple_of(i * 256, 256), 256)
        spec[at, :] = (
            jnp.dot(z_hi[at, :], two_hi[...], preferred_element_type=F32)
            + jnp.dot(z_hi[at, :], two_lo[...], preferred_element_type=F32)
            + jnp.dot(z_lo[at, :], two_hi[...], preferred_element_type=F32)
        )
        return carry

    lax.fori_loop(0, WIDTH // 256, block, 0)


def signal_of(tabs, z_hi, z_lo, spec, rows):
    _, cos_t, sin_t, two_hi, two_lo, last = tabs
    second(z_hi, z_lo, two_hi, two_lo, spec)
    for c in range(CHAN):
        at = slice(c * RANKS, (c + 1) * RANKS)
        re, im = spec[at, :POS], spec[at, POS:]
        hi_re, lo_re = split(re * cos_t[...] - im * sin_t[...])
        hi_im, lo_im = split(re * sin_t[...] + im * cos_t[...])
        stack = jnp.concatenate([hi_re, hi_im, hi_re, hi_im, lo_re, lo_im], 0)
        y = jnp.dot(last[...], stack, preferred_element_type=F32)
        for u in range(2):
            rows[u, pl.ds(c, RANKS, stride=CHAN), :] = y[:, u * 128 : (u + 1) * 128]


def spectral_product(left, right, conj_right, z_hi, z_lo):
    def block(i, carry):
        at = pl.ds(pl.multiple_of(i * 64, 64), 64)
        a, b, c, d = left[at, :POS], left[at, POS:], right[at, :POS], right[at, POS:]
        if conj_right:
            re, im = a * c + b * d, b * c - a * d
        else:
            re, im = a * c - b * d, -(a * d + b * c)
        z_hi[at, :POS], z_lo[at, :POS] = split(re)
        z_hi[at, POS:], z_lo[at, POS:] = split(im)
        return carry

    lax.fori_loop(0, WIDTH // 64, block, 0)


def load_rows(blocks, which, rows):
    for s in range(RANKS):
        for u in range(2):
            rows[u, s * CHAN : (s + 1) * CHAN, :] = blocks[s, which, :, u * 128 : (u + 1) * 128].astype(F32)


def store_rows(rows, blocks, which):
    for s in range(RANKS):
        for u in range(2):
            blocks[s, which, :, u * 128 : (u + 1) * 128] = rows[u, s * CHAN : (s + 1) * CHAN, :].astype(BF16)


def first_transforms(got, one, cos_t, sin_t, two_hi, two_lo, last, spec_g, spec_h, conv, rows, z_hi, z_lo, spec):
    tabs = (one, cos_t, sin_t, two_hi, two_lo, last)
    load_rows(got, 0, rows)
    transform(rows, tabs, z_hi, z_lo, spec_g)
    load_rows(got, 1, rows)
    transform(rows, tabs, z_hi, z_lo, spec_h)
    spectral_product(spec_g, spec_h, False, z_hi, z_lo)
    signal_of(tabs, z_hi, z_lo, spec, rows)
    store_rows(rows, conv, 0)


def second_transforms(got, spec_g, spec_h, one, cos_t, sin_t, two_hi, two_lo, last, out, rows, z_hi, z_lo, spec, spec_d):
    tabs = (one, cos_t, sin_t, two_hi, two_lo, last)
    load_rows(got, 1, rows)
    transform(rows, tabs, z_hi, z_lo, spec_d)
    spectral_product(spec_h, spec_d, True, z_hi, z_lo)
    signal_of(tabs, z_hi, z_lo, spec, rows)
    store_rows(rows, out, 0)
    spectral_product(spec_g, spec_d, True, z_hi, z_lo)
    signal_of(tabs, z_hi, z_lo, spec, rows)
    store_rows(rows, out, 1)


def greet():
    x, y, z, b = coords()
    barrier = pltpu.get_barrier_semaphore()

    def say(e, carry):
        pl.semaphore_signal(barrier, inc=1, device_id=partner(e), device_id_type=MESH)
        return carry

    lax.fori_loop(1, RANKS, say, 0)
    pl.semaphore_wait(barrier, RANKS - 1)


def partner(e):
    x, y, z, b = coords()
    return device((x + e // 16) % 4, (y + (e // 4) % 4) % 4, (z + (e // 2) % 2) % 2, (b + e % 2) % 2)


def block_copy(e, src, got, send_sem, recv_sem):
    there = partner(e)
    return pltpu.make_async_remote_copy(
        src_ref=src.at[there[0]],
        dst_ref=got.at[lax.axis_index("ctx")],
        send_sem=send_sem.at[e],
        recv_sem=recv_sem.at[e],
        device_id=there,
        device_id_type=MESH,
    )


def start_exchange(src, got, send_sem, recv_sem):
    def far(i, carry):
        block_copy((i // 2) * 4 + i % 2 + 2, src, got, send_sem, recv_sem).start()
        return carry

    def near(i, carry):
        block_copy((i // 2) * 4 + i % 2, src, got, send_sem, recv_sem).start()
        return carry

    lax.fori_loop(0, 32, far, 0)
    lax.fori_loop(1, 32, near, 0)
    me = lax.axis_index("ctx")
    got[me] = src[me]


def finish_exchange(src, got, send_sem, recv_sem):
    def end(e, carry):
        block_copy(e, src, got, send_sem, recv_sem).wait()
        return carry

    lax.fori_loop(1, RANKS, end, 0)


def remote(src, dst, there, send_sem, recv_sem):
    return pltpu.make_async_remote_copy(
        src_ref=src, dst_ref=dst, send_sem=send_sem, recv_sem=recv_sem, device_id=there, device_id_type=MESH
    )


def open_kernel(
    in_gate, values, taps, out_gate, shard, out_grad,
    got, grad_y, grad_conv, pair_grad,
    src, weights, turned, send_sem, recv_sem, ag_send, ag_recv, sib_send, sib_recv,
):
    x, y, z, b = coords()
    sibling = device(x, y, z, 1 - b)
    greet()
    weights[x, y, z, b] = shard[...]
    halves = (pl.ds(0, WIDTH // 2), pl.ds(WIDTH // 2, WIDTH // 2))

    def gather(slot, n, there):
        return remote(slot, slot, there, ag_send.at[n], ag_recv.at[n])

    def relay(slot, n):
        return remote(slot, slot, sibling, sib_send.at[n], sib_recv.at[n])

    far = gather(weights.at[x, y, z, b], 0, device(x, y, 1 - z, b))
    far.start()

    for n in range(WIDTH // 128):
        at = slice(n * 128, (n + 1) * 128)
        gated = (in_gate[:, at].astype(F32) * values[:, at].astype(F32)).astype(BF16).astype(F32)
        src[n * 8 : (n + 1) * 8, 0] = gated.T.astype(BF16).reshape(8, CHAN, POS)
        src[n * 8 : (n + 1) * 8, 1] = taps[:, at].astype(F32).T.astype(BF16).reshape(8, CHAN, POS)
    start_exchange(src, got, send_sem, recv_sem)

    relays = [relay(weights.at[x, y, z, b], 0)]
    relays[0].start()
    far.wait()
    stage = []
    for d in range(1, 4):
        stage.append(gather(weights.at[x, y, :, b, :, halves[0]], d, device((x + d) % 4, y, z, b)))
        stage.append(gather(weights.at[x, y, :, b, :, halves[1]], 3 + d, device(x, (y + d) % 4, z, b)))
    for copy in stage:
        copy.start()
    relays.append(relay(weights.at[x, y, 1 - z, b], 1))
    relays[1].start()

    for n in range(MODEL // 128):
        at = slice(n * 128, (n + 1) * 128)
        turned[at, :] = out_grad[:, at].astype(F32).T.astype(BF16)

    def mine(n, carry):
        at = pl.ds(pl.multiple_of(n * 128 + b * 64, 64), 64)
        pair_grad[b, pl.ds(pl.multiple_of(n * 64, 64), 64), :] = turned[at, :]
        return carry

    def theirs(n, carry):
        at = pl.ds(pl.multiple_of(n * 128 + (1 - b) * 64, 64), 64)
        kept = pl.ds(pl.multiple_of(n * 64, 64), 64)
        turned[kept, :] = turned[at, :]
        return carry

    lax.fori_loop(0, MODEL // 128, mine, 0)
    lax.fori_loop(0, MODEL // 128, theirs, 0)
    pair = remote(turned.at[pl.ds(0, MODEL // 2)], pair_grad.at[b], sibling, sib_send.at[14], sib_recv.at[14])
    pair.start()

    for copy in stage:
        copy.wait()
    stage = []
    for d in range(1, 4):
        stage.append(gather(weights.at[:, y, :, b, :, halves[0]], 6 + d, device(x, (y + d) % 4, z, b)))
        stage.append(gather(weights.at[x, :, :, b, :, halves[1]], 9 + d, device((x + d) % 4, y, z, b)))
    for copy in stage:
        copy.start()
    for d in range(1, 4):
        relays.append(relay(weights.at[(x + 4 - d) % 4, y, :, b, :, halves[0]], 1 + d))
        relays.append(relay(weights.at[x, (y + 4 - d) % 4, :, b, :, halves[1]], 4 + d))
    for copy in relays[2:]:
        copy.start()
    last = []
    for d in range(1, 4):
        stage[2 * d - 2].wait()
        last.append(relay(weights.at[:, (y + 4 - d) % 4, :, b, :, halves[0]], 7 + d))
        last[-1].start()
        stage[2 * d - 1].wait()
        last.append(relay(weights.at[(x + 4 - d) % 4, :, :, b, :, halves[1]], 10 + d))
        last[-1].start()
    for copy in relays + last:
        copy.wait()

    for n in range(WIDTH // 256):
        at = slice(n * 256, (n + 1) * 256)
        right = weights[:, :, :, :, :, at].reshape(MODEL, 256)
        product = jnp.dot(out_grad[...], right, preferred_element_type=F32).astype(BF16)
        grad_y[:, at] = product
        turned_gate = (product.astype(F32) * out_gate[:, at].astype(F32)).astype(BF16).astype(F32)
        grad_conv[n * 16 : (n + 1) * 16] = turned_gate.T.astype(BF16).reshape(16, CHAN, POS)
    pair.wait()
    finish_exchange(src, got, send_sem, recv_sem)


def middle_kernel(conv, grad_conv, got, src, send_sem, recv_sem):
    greet()
    for s in range(RANKS):
        src[s, 0] = conv[s, 0]
        src[s, 1] = grad_conv[s]
    start_exchange(src, got, send_sem, recv_sem)
    finish_exchange(src, got, send_sem, recv_sem)


def close_kernel(
    src, mixed, pair_grad,
    got, weight_grad,
    pair_mixed, send_one, recv_one, send_two, recv_two, send_three, recv_three, own,
    send_sem, recv_sem, rs_send, rs_recv,
):
    x, y, z, b = coords()
    sibling = device(x, y, z, 1 - b)
    greet()
    pair = remote(mixed, pair_mixed.at[b], sibling, rs_send.at[0], rs_recv.at[0])
    pair.start()
    start_exchange(src, got, send_sem, recv_sem)
    pair_mixed[b] = mixed[...]
    pair.wait()
    half = WIDTH // 2

    def partial(first_row, count, at):
        rows = pl.ds(pl.multiple_of(first_row, 128), count)
        return jnp.dot(pair_grad[0, rows, :], pair_mixed[0, :, at], preferred_element_type=F32) + jnp.dot(
            pair_grad[1, rows, :], pair_mixed[1, :, at], preferred_element_type=F32
        )

    lanes = (slice(0, half), slice(half, WIDTH))
    stage = []
    for d in (2, 1, 3):
        to = (x + d) % 4
        send_one[0, d - 1] = partial(to * 512, 512, lanes[0]).astype(BF16)
        copy = remote(send_one.at[0, d - 1], recv_one.at[0, d - 1], device(to, y, z, b), rs_send.at[d], rs_recv.at[d])
        copy.start()
        stage.append(copy)
        to = (y + d) % 4
        for u in range(4):
            send_one[1, d - 1, u * 128 : (u + 1) * 128, :] = partial(u * 512 + to * 128, 128, lanes[1]).astype(BF16)
        copy = remote(
            send_one.at[1, d - 1], recv_one.at[1, d - 1], device(x, to, z, b), rs_send.at[3 + d], rs_recv.at[3 + d]
        )
        copy.start()
        stage.append(copy)
    own[0] = partial(x * 512, 512, lanes[0])
    for u in range(4):
        own[1, u * 128 : (u + 1) * 128, :] = partial(u * 512 + y * 128, 128, lanes[1])
    for copy in stage:
        copy.wait()

    def summed(h, place):
        at = pl.ds(pl.multiple_of(place * 128, 128), 128)
        total = own[h, at, :]
        for d in range(3):
            total = total + recv_one[h, d, at, :].astype(F32)
        return total

    stage = []
    for d in (2, 1, 3):
        to = (y + d) % 4
        send_two[0, d - 1] = summed(0, to).astype(BF16)
        copy = remote(
            send_two.at[0, d - 1], recv_two.at[0, d - 1], device(x, to, z, b), rs_send.at[6 + d], rs_recv.at[6 + d]
        )
        copy.start()
        stage.append(copy)
        to = (x + d) % 4
        send_two[1, d - 1] = summed(1, to).astype(BF16)
        copy = remote(
            send_two.at[1, d - 1], recv_two.at[1, d - 1], device(to, y, z, b), rs_send.at[9 + d], rs_recv.at[9 + d]
        )
        copy.start()
        stage.append(copy)
    own[0, 0:128, :] = summed(0, y)
    own[1, 0:128, :] = summed(1, x)
    for copy in stage:
        copy.wait()
    for h in range(2):
        total = own[h, 0:128, :]
        for d in range(3):
            total = total + recv_two[h, d].astype(F32)
        own[h, 0:128, :] = total
    there = pl.ds(pl.multiple_of((1 - z) * 64, 64), 64)
    here = pl.ds(pl.multiple_of(z * 64, 64), 64)
    send_three[0] = own[0, there, :].astype(BF16)
    send_three[1] = own[1, there, :].astype(BF16)
    copy = remote(send_three, recv_three, device(x, y, 1 - z, b), rs_send.at[13], rs_recv.at[13])
    copy.start()
    copy.wait()
    for h in range(2):
        weight_grad[:, lanes[h]] = own[h, here, :] + recv_three[h].astype(F32)
    finish_exchange(src, got, send_sem, recv_sem)


BLOCKS = jax.ShapeDtypeStruct((RANKS, 2, CHAN, POS), BF16)
WHOLE = pl.BlockSpec(memory_space=pltpu.VMEM)
DMA = pltpu.SemaphoreType.DMA


def call(body, name, operands, outs, scratch, collective_id=None):
    if collective_id is None:
        params = pltpu.CompilerParams(vmem_limit_bytes=VMEM_LIMIT)
    else:
        params = pltpu.CompilerParams(
            collective_id=collective_id, has_side_effects=True, vmem_limit_bytes=VMEM_LIMIT
        )
    return pl.pallas_call(
        body,
        name=name,
        out_shape=outs,
        in_specs=[WHOLE] * len(operands),
        out_specs=[WHOLE] * len(outs),
        scratch_shapes=scratch,
        compiler_params=params,
    )(*operands)


def product(left, right):
    return (left.astype(F32) * right.astype(F32)).astype(BF16)


def on_device(out_gate, in_gate, values, filter_taps, out_grad, out_weight):
    tabs = [jnp.asarray(table) for table in tables()]
    shape = jax.ShapeDtypeStruct
    sems = [DMA((RANKS,)), DMA((RANKS,))]
    got_one, grad_y, grad_conv, pair_grad = call(
        open_kernel,
        "open_kernel",
        (in_gate, values, filter_taps, out_gate, out_weight.T, out_grad),
        [BLOCKS, shape((POS, WIDTH), BF16), shape((RANKS, CHAN, POS), BF16), shape((2, MODEL // 2, POS), BF16)],
        [
            pltpu.VMEM(BLOCKS.shape, BF16),
            pltpu.VMEM((4, 4, 2, 2, 64, WIDTH), BF16),
            pltpu.VMEM((MODEL, POS), BF16),
        ]
        + sems
        + [DMA((13,)), DMA((13,)), DMA((15,)), DMA((15,))],
        0,
    )
    spectrum = shape((WIDTH, 2 * POS), F32)
    work = [
        pltpu.VMEM((2, WIDTH, 128), F32),
        pltpu.VMEM((WIDTH, 2 * POS), BF16),
        pltpu.VMEM((WIDTH, 2 * POS), BF16),
        pltpu.VMEM((WIDTH, 2 * POS), F32),
    ]
    spec_g, spec_h, conv_blocks = call(
        first_transforms,
        "first_transforms",
        (got_one, *tabs),
        [spectrum, spectrum, shape((RANKS, 1, CHAN, POS), BF16)],
        work,
    )
    (got_two,) = call(
        middle_kernel, "middle_kernel", (conv_blocks, grad_conv), [BLOCKS], [pltpu.VMEM(BLOCKS.shape, BF16)] + sems, 1
    )
    (src_three,) = call(
        second_transforms,
        "second_transforms",
        (got_two, spec_g, spec_h, *tabs),
        [BLOCKS],
        work + [pltpu.VMEM((WIDTH, 2 * POS), F32)],
    )
    conv = got_two[:, 0].reshape(WIDTH, POS).T
    half = WIDTH // 2
    got_three, weight_grad = call(
        close_kernel,
        "close_kernel",
        (src_three, product(out_gate, conv), pair_grad),
        [BLOCKS, shape((64, WIDTH), F32)],
        [
            pltpu.VMEM((2, POS, WIDTH), BF16),
            pltpu.VMEM((2, 3, 512, half), BF16),
            pltpu.VMEM((2, 3, 512, half), BF16),
            pltpu.VMEM((2, 3, 128, half), BF16),
            pltpu.VMEM((2, 3, 128, half), BF16),
            pltpu.VMEM((2, 64, half), BF16),
            pltpu.VMEM((2, 64, half), BF16),
            pltpu.VMEM((2, 512, half), F32),
        ]
        + sems
        + [DMA((14,)), DMA((14,))],
        2,
    )
    grad_gated = got_three[:, 0].reshape(WIDTH, POS).T
    taps_grad = got_three[:, 1].reshape(WIDTH, POS).T.astype(F32)
    return (
        product(grad_y, conv),
        product(grad_gated, values),
        product(grad_gated, in_gate),
        taps_grad,
        weight_grad.T,
    )


def solution(mesh):
    return jax.shard_map(
        on_device,
        mesh=mesh,
        in_specs=(
            P("ctx", "ch"),
            P("ctx", "ch"),
            P("ctx", "ch"),
            P("ctx", "ch"),
            P("ctx", None),
            P("ch", "ctx"),
        ),
        out_specs=(P("ctx", "ch"), P("ctx", "ch"), P("ctx", "ch"), P("ctx", "ch"), P("ch", "ctx")),
        check_vma=False,
    )
```

time: 855 us -> 213 us (0.25)
  the two profiles are of different devices: /device:TPU:32 before, /device:TPU:64 now
where the time goes in v1:
time: 213 us
  Pallas kernels  205 us (96%)
  local copies, waits for them, and re-layouts  4.72 us (2%)
  other arithmetic  2.87 us (1%)
    pallas_call x5, Pallas kernels, call(): pl.pallas_call(body, name=name, out_shape=outs, in_specs=[WHOLE] * len(op...  205 us

profile of v1, /device:TPU:64, one launch (start us, length us, event | category | flops | bytes accessed | tf_op | source)
XLA Modules:
  0.0 213.2 jit_solution(17543713126357496361)
XLA Ops:
  0.6 77.1 %open_kernel.1 = (bf16[64,2,16,256]{3,2,1,0:T(8,128)(2,1)}, bf16[256,1024]{1,0:T(8,128)(2,1)}, bf16[64,16,256]{2,1,0:T(8,128)(2,1)}, bf16[2,2048,256]{2,1,0:T(8,128)(2,1)}) custom-call(bf16[256,1024]{1,0:T(8,128)(2,1)} %in_gate.1, bf16[256,1024]{1,0:T(8,128)(2,1)} %values.1, bf16[256,1024]{1,0:T(8,128)(2,1)} %taps.1, bf16[256,1024]{1,0:T(8,128)(2,1)} %out_gate.1, ...), custom_call_target="tpu_custom_call" | custom-call | tf_op jit(solution)/shard_map/open_kernel/pallas_call | solution.py:418
  77.7 12.8 %first_transforms.1 = (f32[1024,512]{1,0:T(8,128)}, f32[1024,512]{1,0:T(8,128)}, bf16[64,1,16,256]{3,2,1,0:T(8,128)(2,1)}) custom-call(bf16[64,2,16,256]{3,2,1,0:T(8,128)(2,1)} %get-tuple-element.15.got, bf16[128,128]{1,0:T(8,128)(2,1)} %constant.12.clone.one, f32[64,256]{1,0:T(8,128)} %constant.13.clone.cos_t, f32[64,256]{1,0:T(8,128)} %constant.14.clone.sin_t, ...), custom_call_target="tpu_custom_call" | custom-call | tf_op jit(solution)/shard_map/first_transforms/pallas_call | solution.py:418
  90.5 34.1 %middle_kernel.1.got = bf16[64,2,16,256]{3,2,1,0:T(8,128)(2,1)} custom-call(bf16[64,1,16,256]{3,2,1,0:T(8,128)(2,1)} %get-tuple-element.16.conv, bf16[64,16,256]{2,1,0:T(8,128)(2,1)} %get-tuple-element.17.grad_conv), custom_call_target="tpu_custom_call" | custom-call | tf_op jit(solution)/shard_map/middle_kernel/pallas_call | solution.py:418
  124.7 0.0 slice-start
  124.7 15.0 %second_transforms.1.src = bf16[64,2,16,256]{3,2,1,0:T(8,128)(2,1)} custom-call(bf16[64,2,16,256]{3,2,1,0:T(8,128)(2,1)} %middle_kernel.1.got, f32[1024,512]{1,0:T(8,128)} %get-tuple-element.18.spec_g, f32[1024,512]{1,0:T(8,128)} %get-tuple-element.19.spec_h, bf16[128,128]{1,0:T(8,128)(2,1)} %constant.12.clone.one, f32[64,256]{1,0:T(8,128)} %constant.13.clone.cos_t, ...), custom_call_target="tpu_custom_call" | custom-call | tf_op jit(solution)/shard_map/second_transforms/pallas_call | solution.py:418
  139.7 0.0 slice-done
  139.7 0.0 copy-start
  139.7 0.0 copy-start.3
  139.7 0.1 bitcast_convert_fusion.2
  139.8 0.3 copy.20
  140.2 0.6 copy-done
  140.8 0.2 copy-done.3
  140.9 1.3 fusion.3
  142.2 65.8 %close_kernel.1 = (bf16[64,2,16,256]{3,2,1,0:T(8,128)(2,1)}, f32[64,1024]{1,0:T(8,128)}) custom-call(bf16[64,2,16,256]{3,2,1,0:T(8,128)(2,1)} %second_transforms.1.src, bf16[256,1024]{1,0:T(8,128)(2,1)} %get-tuple-element.27.mixed, bf16[2,2048,256]{2,1,0:T(8,128)(2,1)} %get-tuple-element.20.pair_grad), custom_call_target="tpu_custom_call" | custom-call | tf_op jit(solution)/shard_map/close_kernel/pallas_call | solution.py:418
  208.0 1.3 fusion.4
  209.2 0.2 bitcast_convert_fusion
  209.5 0.0 copy-start.1
  209.5 0.0 copy-start.2
  209.5 1.3 copy.22
  210.8 0.3 copy.21
  211.2 0.0 copy-done.1
  211.2 0.0 copy-done.2
  211.2 0.0 copy-start.4
  211.2 1.3 fusion.1
  212.5 0.0 copy-done.4
  212.5 0.7 copy.24
Async XLA Ops:
  124.7 15.1 %slice-start = ((bf16[64,2,16,256]{3,2,1,0:T(8,128)(2,1)}), bf16[64,1,16,256]{3,2,1,0:T(8,128)(2,1)S(1)}, s32[]{:S(2)}) async-start(bf16[64,2,16,256]{3,2,1,0:T(8,128)(2,1)} %middle_kernel.1.got), calls=%async_computation | async-start | bytes 1048576 | tf_op jit(solution)/shard_map/slice | solution.py:475
  139.7 1.0 copy-start
  139.7 1.2 copy-start.3
  209.5 1.7 copy-start.1
  209.5 1.7 copy-start.2
  211.2 1.3 copy-start.4

commit v2 on v1

v2 whole, which is shorter than its diff:
```python
import functools

import jax
import jax.numpy as jnp
import numpy as np
from jax import lax
from jax.experimental import pallas as pl
from jax.experimental.pallas import tpu as pltpu
from jax.sharding import PartitionSpec as P

MESH = pl.DeviceIdType.MESH
F32 = jnp.float32
BF16 = jnp.bfloat16

RANKS = 64
POS = 256
CHAN = 16
WIDTH = RANKS * CHAN
MODEL = 4096
VMEM_LIMIT = 60 * 2**20


def coords():
    i = lax.axis_index("ctx")
    return i // 16, (i // 4) % 4, (i // 2) % 2, i % 2


def device(x, y, z, b):
    return (((x * 4 + y) * 2 + z) * 2 + b, lax.axis_index("ch"))


def split(x):
    hi = x.astype(BF16)
    return hi, (x - hi.astype(F32)).astype(BF16)


def tables():
    n = RANKS * POS
    k1 = np.arange(RANKS) + 0.25
    first = 2 * np.pi * k1[:, None] * np.arange(RANKS)[None, :] / RANKS
    turn = 2 * np.pi * k1[:, None] * np.arange(POS)[None, :] / n
    second = 2 * np.pi * ((np.arange(POS)[:, None] * np.arange(POS)[None, :]) % POS) / POS

    def parts(table):
        hi = table.astype(jnp.bfloat16)
        lo = (table - hi.astype(np.float64)).astype(jnp.bfloat16)
        return hi, lo

    one = np.concatenate([np.cos(first), -np.sin(first)], 0)
    one_hi, one_lo = parts(one)
    cos, sin = np.cos(second), np.sin(second)
    two_hi, two_lo = parts(np.block([[cos, -sin], [sin, cos]]))
    last = np.concatenate([np.cos(first), np.sin(first)], 0).T / n
    last_hi, last_lo = parts(last)
    return (
        np.concatenate([one_hi, one_lo], 1),
        np.cos(turn).astype(np.float32),
        (-np.sin(turn)).astype(np.float32),
        two_hi,
        two_lo,
        np.concatenate([last_hi, last_lo, last_hi], 1),
    )


def transform(rows, tabs, z_hi, z_lo, spec):
    one, cos_t, sin_t, two_hi, two_lo, _ = tabs
    for c in range(CHAN):
        x = jnp.concatenate([rows[u, pl.ds(c, RANKS, stride=CHAN), :] for u in range(2)], 1).astype(BF16)
        a = jnp.dot(one[...], jnp.concatenate([x, x], 0), preferred_element_type=F32)
        turn_in(a[:RANKS], a[RANKS:], cos_t, sin_t, z_hi, z_lo, c)
    second(z_hi, z_lo, two_hi, two_lo, spec)


def turn_in(re, im, cos_t, sin_t, z_hi, z_lo, c):
    at = slice(c * RANKS, (c + 1) * RANKS)
    z_hi[at, :POS], z_lo[at, :POS] = split(re * cos_t[...] - im * sin_t[...])
    z_hi[at, POS:], z_lo[at, POS:] = split(re * sin_t[...] + im * cos_t[...])


def second(z_hi, z_lo, two_hi, two_lo, spec):
    def block(i, carry):
        at = pl.ds(pl.multiple_of(i * 256, 256), 256)
        spec[at, :] = (
            jnp.dot(z_hi[at, :], two_hi[...], preferred_element_type=F32)
            + jnp.dot(z_hi[at, :], two_lo[...], preferred_element_type=F32)
            + jnp.dot(z_lo[at, :], two_hi[...], preferred_element_type=F32)
        )
        return carry

    lax.fori_loop(0, WIDTH // 256, block, 0)


def signal_of(tabs, z_hi, z_lo, spec, rows):
    _, cos_t, sin_t, two_hi, two_lo, last = tabs
    second(z_hi, z_lo, two_hi, two_lo, spec)
    for c in range(CHAN):
        at = slice(c * RANKS, (c + 1) * RANKS)
        re, im = spec[at, :POS], spec[at, POS:]
        hi_re, lo_re = split(re * cos_t[...] - im * sin_t[...])
        hi_im, lo_im = split(re * sin_t[...] + im * cos_t[...])
        stack = jnp.concatenate([hi_re, hi_im, hi_re, hi_im, lo_re, lo_im], 0)
        y = jnp.dot(last[...], stack, preferred_element_type=F32)
        for u in range(2):
            rows[u, pl.ds(c, RANKS, stride=CHAN), :] = y[:, u * 128 : (u + 1) * 128]


def spectral_product(left, right, conj_right, z_hi, z_lo):
    def block(i, carry):
        at = pl.ds(pl.multiple_of(i * 64, 64), 64)
        a, b, c, d = left[at, :POS], left[at, POS:], right[at, :POS], right[at, POS:]
        if conj_right:
            re, im = a * c + b * d, b * c - a * d
        else:
            re, im = a * c - b * d, -(a * d + b * c)
        z_hi[at, :POS], z_lo[at, :POS] = split(re)
        z_hi[at, POS:], z_lo[at, POS:] = split(im)
        return carry

    lax.fori_loop(0, WIDTH // 64, block, 0)


def load_rows(blocks, rows):
    for s in range(RANKS):
        for u in range(2):
            rows[u, s * CHAN : (s + 1) * CHAN, :] = blocks[s, :, u * 128 : (u + 1) * 128].astype(F32)


def store_rows(rows, blocks):
    for s in range(RANKS):
        for u in range(2):
            blocks[s, :, u * 128 : (u + 1) * 128] = rows[u, s * CHAN : (s + 1) * CHAN, :].astype(BF16)


def partner(e):
    x, y, z, b = coords()
    return device((x + e // 16) % 4, (y + (e // 4) % 4) % 4, (z + (e // 2) % 2) % 2, (b + e % 2) % 2)


def remote(src, dst, there, send_sem, recv_sem):
    return pltpu.make_async_remote_copy(
        src_ref=src, dst_ref=dst, send_sem=send_sem, recv_sem=recv_sem, device_id=there, device_id_type=MESH
    )


def start_exchange(src, got, send_sem, recv_sem):
    me = lax.axis_index("ctx")

    def send(e):
        there = partner(e)
        remote(src.at[there[0]], got.at[me], there, send_sem, recv_sem).start()

    def far(i, carry):
        send((i // 2) * 4 + i % 2 + 2)
        return carry

    def near(i, carry):
        send((i // 2) * 4 + i % 2)
        return carry

    lax.fori_loop(0, 32, far, 0)
    lax.fori_loop(1, 32, near, 0)
    got[me] = src[me]


def finish(blocks, sem):
    others = blocks.at[pl.ds(0, RANKS - 1)]
    pltpu.make_async_copy(others, others, sem).wait()


def kernel(
    in_gate, values, taps, out_gate, shard, out_grad, one, cos_t, sin_t, two_hi, two_lo, last,
    out_gate_grad, got_gg, got_tg, weight_grad,
    src_in, got_g, got_h, src_h, src_c, got_c, src_d, got_d, src_gg, src_tg,
    weights, turned, pair_grad, grad_y,
    rows, z_hi, z_lo, spec, spec_g, spec_h,
    pair_mixed, send_one, recv_one, send_two, recv_two, send_three, recv_three, own,
    ex_send, ex_recv, ag_send, ag_recv, sib_send, sib_recv, rs_send, rs_recv,
):
    x, y, z, b = coords()
    sibling = device(x, y, z, 1 - b)
    tabs = (one, cos_t, sin_t, two_hi, two_lo, last)
    half = WIDTH // 2
    halves = (pl.ds(0, half), pl.ds(half, half))
    sent = []

    barrier = pltpu.get_barrier_semaphore()

    def say(e, carry):
        pl.semaphore_signal(barrier, inc=1, device_id=partner(e), device_id_type=MESH)
        return carry

    lax.fori_loop(1, RANKS, say, 0)
    weights[x, y, z, b] = shard[...]
    for n in range(WIDTH // 128):
        at = slice(n * 128, (n + 1) * 128)
        gated = (in_gate[:, at].astype(F32) * values[:, at].astype(F32)).astype(BF16).astype(F32)
        src_in[n * 8 : (n + 1) * 8] = gated.T.astype(BF16).reshape(8, CHAN, POS)
        src_h[n * 8 : (n + 1) * 8] = taps[:, at].astype(F32).T.astype(BF16).reshape(8, CHAN, POS)
    pl.semaphore_wait(barrier, RANKS - 1)

    def gather(slot, n, there):
        copy = remote(slot, slot, there, ag_send.at[n], ag_recv.at[n])
        copy.start()
        sent.append(copy)
        return copy

    relays = []

    def relay(slot):
        n = len(relays)
        copy = remote(slot, slot, sibling, sib_send.at[n], sib_recv.at[n])
        copy.start()
        sent.append(copy)
        relays.append(copy)

    def first_round(plane, n):
        stage = []
        for d in (2, 1, 3):
            stage.append(gather(weights.at[x, y, plane, b, :, halves[0]], n + d, device((x + d) % 4, y, z, b)))
            stage.append(gather(weights.at[x, y, plane, b, :, halves[1]], n + 3 + d, device(x, (y + d) % 4, z, b)))
        relay(weights.at[x, y, plane, b])
        return stage

    def second_round(plane, n, stage):
        for copy in stage:
            copy.wait_recv()
        stage = []
        for d in (2, 1, 3):
            stage.append(gather(weights.at[:, y, plane, b, :, halves[0]], n + d, device(x, (y + d) % 4, z, b)))
            stage.append(gather(weights.at[x, :, plane, b, :, halves[1]], n + 3 + d, device((x + d) % 4, y, z, b)))
        for d in (2, 1, 3):
            relay(weights.at[(x + 4 - d) % 4, y, plane, b, :, halves[0]])
            relay(weights.at[x, (y + 4 - d) % 4, plane, b, :, halves[1]])
        return stage

    def last_round(plane, stage):
        for n, d in enumerate((2, 1, 3)):
            stage[2 * n].wait_recv()
            relay(weights.at[:, (y + 4 - d) % 4, plane, b, :, halves[0]])
            stage[2 * n + 1].wait_recv()
            relay(weights.at[(x + 4 - d) % 4, :, plane, b, :, halves[1]])

    far = gather(weights.at[x, y, z, b], 0, device(x, y, 1 - z, b))
    near_stage = first_round(z, 0)
    start_exchange(src_in, got_g, ex_send.at[0], ex_recv.at[0])
    start_exchange(src_h, got_h, ex_send.at[1], ex_recv.at[1])
    far.wait_recv()
    far_stage = first_round(1 - z, 6)

    for n in range(MODEL // 128):
        at = slice(n * 128, (n + 1) * 128)
        turned[at, :] = out_grad[:, at].astype(F32).T.astype(BF16)

    near_stage = second_round(z, 12, near_stage)

    def mine(n, carry):
        at = pl.ds(pl.multiple_of(n * 128 + b * 64, 64), 64)
        pair_grad[b, pl.ds(pl.multiple_of(n * 64, 64), 64), :] = turned[at, :]
        return carry

    def theirs(n, carry):
        at = pl.ds(pl.multiple_of(n * 128 + (1 - b) * 64, 64), 64)
        kept = pl.ds(pl.multiple_of(n * 64, 64), 64)
        turned[kept, :] = turned[at, :]
        return carry

    lax.fori_loop(0, MODEL // 128, mine, 0)
    lax.fori_loop(0, MODEL // 128, theirs, 0)
    pair = remote(turned.at[pl.ds(0, MODEL // 2)], pair_grad.at[b], sibling, rs_send.at[14], rs_recv.at[14])
    pair.start()
    sent.append(pair)

    far_stage = second_round(1 - z, 18, far_stage)

    finish(got_g, ex_recv.at[0])
    load_rows(got_g, rows)
    transform(rows, tabs, z_hi, z_lo, spec_g)
    finish(got_h, ex_recv.at[1])
    load_rows(got_h, rows)
    transform(rows, tabs, z_hi, z_lo, spec_h)
    last_round(z, near_stage)
    spectral_product(spec_g, spec_h, False, z_hi, z_lo)
    signal_of(tabs, z_hi, z_lo, spec, rows)
    store_rows(rows, src_c)
    start_exchange(src_c, got_c, ex_send.at[2], ex_recv.at[2])

    last_round(1 - z, far_stage)
    for copy in relays:
        copy.wait_recv()
    for n in range(WIDTH // 256):
        at = slice(n * 256, (n + 1) * 256)
        right = weights[:, :, :, :, :, at].reshape(MODEL, 256)
        product = jnp.dot(out_grad[...], right, preferred_element_type=F32).astype(BF16)
        grad_y[:, at] = product
        grad_conv = (product.astype(F32) * out_gate[:, at].astype(F32)).astype(BF16).astype(F32)
        src_d[n * 16 : (n + 1) * 16] = grad_conv.T.astype(BF16).reshape(16, CHAN, POS)
    start_exchange(src_d, got_d, ex_send.at[3], ex_recv.at[3])

    finish(got_c, ex_recv.at[2])
    for n in range(WIDTH // 128):
        at = slice(n * 128, (n + 1) * 128)
        conv = got_c[n * 8 : (n + 1) * 8].reshape(128, POS).astype(F32).T
        pair_mixed[b, :, at] = (out_gate[:, at].astype(F32) * conv).astype(BF16)
        out_gate_grad[:, at] = (grad_y[:, at].astype(F32) * conv).astype(BF16)
    mixed = remote(pair_mixed.at[b], pair_mixed.at[b], sibling, rs_send.at[0], rs_recv.at[0])
    mixed.start()
    sent.append(mixed)

    def partial(first_row, count, at):
        at_rows = pl.ds(pl.multiple_of(first_row, 128), count)
        return jnp.dot(pair_grad[0, at_rows, :], pair_mixed[0, :, at], preferred_element_type=F32) + jnp.dot(
            pair_grad[1, at_rows, :], pair_mixed[1, :, at], preferred_element_type=F32
        )

    def reduce_to(src, dst, n, there):
        copy = remote(src, dst, there, rs_send.at[n], rs_recv.at[n])
        copy.start()
        sent.append(copy)
        return copy

    pair.wait_recv()
    mixed.wait_recv()
    lanes = (slice(0, half), slice(half, WIDTH))
    stage = []
    for d in (2, 1, 3):
        to = (x + d) % 4
        send_one[0, d - 1] = partial(to * 512, 512, lanes[0]).astype(BF16)
        stage.append(reduce_to(send_one.at[0, d - 1], recv_one.at[0, d - 1], d, device(to, y, z, b)))
        to = (y + d) % 4
        for u in range(4):
            send_one[1, d - 1, u * 128 : (u + 1) * 128, :] = partial(u * 512 + to * 128, 128, lanes[1]).astype(BF16)
        stage.append(reduce_to(send_one.at[1, d - 1], recv_one.at[1, d - 1], 3 + d, device(x, to, z, b)))
    own[0] = partial(x * 512, 512, lanes[0])
    for u in range(4):
        own[1, u * 128 : (u + 1) * 128, :] = partial(u * 512 + y * 128, 128, lanes[1])

    finish(got_d, ex_recv.at[3])
    load_rows(got_d, rows)
    spec_d = spec
    transform(rows, tabs, z_hi, z_lo, spec_d)
    spectral_product(spec_h, spec_d, True, z_hi, z_lo)
    signal_of(tabs, z_hi, z_lo, spec_h, rows)
    store_rows(rows, src_gg)
    start_exchange(src_gg, got_gg, ex_send.at[4], ex_recv.at[4])
    spectral_product(spec_g, spec_d, True, z_hi, z_lo)
    signal_of(tabs, z_hi, z_lo, spec_h, rows)
    store_rows(rows, src_tg)
    start_exchange(src_tg, got_tg, ex_send.at[5], ex_recv.at[5])

    for copy in stage:
        copy.wait_recv()

    def summed(h, place):
        at = pl.ds(pl.multiple_of(place * 128, 128), 128)
        total = own[h, at, :]
        for d in range(3):
            total = total + recv_one[h, d, at, :].astype(F32)
        return total

    stage = []
    for d in (2, 1, 3):
        to = (y + d) % 4
        send_two[0, d - 1] = summed(0, to).astype(BF16)
        stage.append(reduce_to(send_two.at[0, d - 1], recv_two.at[0, d - 1], 6 + d, device(x, to, z, b)))
        to = (x + d) % 4
        send_two[1, d - 1] = summed(1, to).astype(BF16)
        stage.append(reduce_to(send_two.at[1, d - 1], recv_two.at[1, d - 1], 9 + d, device(to, y, z, b)))
    own[0, 0:128, :] = summed(0, y)
    own[1, 0:128, :] = summed(1, x)
    for copy in stage:
        copy.wait_recv()
    for h in range(2):
        total = own[h, 0:128, :]
        for d in range(3):
            total = total + recv_two[h, d].astype(F32)
        own[h, 0:128, :] = total
    there = pl.ds(pl.multiple_of((1 - z) * 64, 64), 64)
    here = pl.ds(pl.multiple_of(z * 64, 64), 64)
    send_three[0] = own[0, there, :].astype(BF16)
    send_three[1] = own[1, there, :].astype(BF16)
    reduce_to(send_three, recv_three, 13, device(x, y, 1 - z, b)).wait_recv()
    for h in range(2):
        weight_grad[:, lanes[h]] = own[h, here, :] + recv_three[h].astype(F32)

    finish(got_gg, ex_recv.at[4])
    finish(got_tg, ex_recv.at[5])
    for n, blocks in enumerate((src_in, src_h, src_c, src_d, src_gg, src_tg)):
        finish(blocks, ex_send.at[n])
    for copy in sent:
        copy.wait_send()


WHOLE = pl.BlockSpec(memory_space=pltpu.VMEM)
DMA = pltpu.SemaphoreType.DMA


def product(left, right):
    return (left.astype(F32) * right.astype(F32)).astype(BF16)


def on_device(out_gate, in_gate, values, filter_taps, out_grad, out_weight):
    tabs = [jnp.asarray(table) for table in tables()]
    shape = jax.ShapeDtypeStruct
    half = WIDTH // 2
    blocks = (RANKS, CHAN, POS)
    operands = (in_gate, values, filter_taps, out_gate, out_weight.T, out_grad, *tabs)
    outs = [shape((POS, WIDTH), BF16), shape(blocks, BF16), shape(blocks, BF16), shape((64, WIDTH), F32)]
    out_gate_grad, got_gg, got_tg, weight_grad = pl.pallas_call(
        kernel,
        name="hyena_backward",
        out_shape=outs,
        in_specs=[WHOLE] * len(operands),
        out_specs=[WHOLE] * len(outs),
        scratch_shapes=[pltpu.VMEM(blocks, BF16) for _ in range(10)]
        + [
            pltpu.VMEM((4, 4, 2, 2, 64, WIDTH), BF16),
            pltpu.VMEM((MODEL, POS), BF16),
            pltpu.VMEM((2, MODEL // 2, POS), BF16),
            pltpu.VMEM((POS, WIDTH), BF16),
            pltpu.VMEM((2, WIDTH, 128), F32),
            pltpu.VMEM((WIDTH, 2 * POS), BF16),
            pltpu.VMEM((WIDTH, 2 * POS), BF16),
            pltpu.VMEM((WIDTH, 2 * POS), F32),
            pltpu.VMEM((WIDTH, 2 * POS), F32),
            pltpu.VMEM((WIDTH, 2 * POS), F32),
            pltpu.VMEM((2, POS, WIDTH), BF16),
            pltpu.VMEM((2, 3, 512, half), BF16),
            pltpu.VMEM((2, 3, 512, half), BF16),
            pltpu.VMEM((2, 3, 128, half), BF16),
            pltpu.VMEM((2, 3, 128, half), BF16),
            pltpu.VMEM((2, 64, half), BF16),
            pltpu.VMEM((2, 64, half), BF16),
            pltpu.VMEM((2, 512, half), F32),
            DMA((6,)),
            DMA((6,)),
            DMA((25,)),
            DMA((25,)),
            DMA((26,)),
            DMA((26,)),
            DMA((15,)),
            DMA((15,)),
        ],
        compiler_params=pltpu.CompilerParams(
            collective_id=0, has_side_effects=True, vmem_limit_bytes=VMEM_LIMIT
        ),
    )(*operands)
    grad_gated = got_gg.reshape(WIDTH, POS).T
    taps_grad = got_tg.reshape(WIDTH, POS).T.astype(F32)
    return (
        out_gate_grad,
        product(grad_gated, values),
        product(grad_gated, in_gate),
        taps_grad,
        weight_grad.T,
    )


def solution(mesh):
    return jax.shard_map(
        on_device,
        mesh=mesh,
        in_specs=(
            P("ctx", "ch"),
            P("ctx", "ch"),
            P("ctx", "ch"),
            P("ctx", "ch"),
            P("ctx", None),
            P("ch", "ctx"),
        ),
        out_specs=(P("ctx", "ch"), P("ctx", "ch"), P("ctx", "ch"), P("ctx", "ch"), P("ch", "ctx")),
        check_vma=False,
    )
```

time: 213 us -> 135 us (0.63)
  Pallas kernels: 205 us -> 128 us
    pallas_call x5 -> x1, Pallas kernels: 205 us -> 128 us  [on_device(): pl.pallas_call(kernel, name='hyena_backward', out_shape=outs, in_specs=[W...]
where the time goes in v2:
time: 135 us
  Pallas kernels  128 us (95%)
  local copies, waits for them, and re-layouts  3.15 us (2%)
  other arithmetic  2.63 us (2%)
    pallas_call x1, Pallas kernels, on_device(): pl.pallas_call(kernel, name='hyena_backward', out_shape=outs, in_specs=[W...  128 us

profile of v2, /device:TPU:64, one launch (start us, length us, event | category | flops | bytes accessed | tf_op | source)
XLA Modules:
  0.0 134.6 jit_solution(16896685946299446801)
XLA Ops:
  0.6 128.1 %hyena_backward.1 = (bf16[256,1024]{1,0:T(8,128)(2,1)}, bf16[64,16,256]{2,1,0:T(8,128)(2,1)}, bf16[64,16,256]{2,1,0:T(8,128)(2,1)}, f32[64,1024]{1,0:T(8,128)}) custom-call(bf16[256,1024]{1,0:T(8,128)(2,1)} %in_gate.1, bf16[256,1024]{1,0:T(8,128)(2,1)} %values.1, bf16[256,1024]{1,0:T(8,128)(2,1)} %taps.1, bf16[256,1024]{1,0:T(8,128)(2,1)} %out_gate.1, ...), custom_call_target="tpu_custom_call" | custom-call | tf_op jit(solution)/shard_map/hyena_backward/pallas_call | solution.py:408
  128.7 1.4 %bitcast_convert_fusion = (f32[1024,256]{1,0:T(8,128)S(1)}, f32[1024,256]{1,0:T(8,128)S(1)}) fusion(bf16[64,16,256]{2,1,0:T(8,128)(2,1)} %get-tuple-element.11, bf16[64,16,256]{2,1,0:T(8,128)(2,1)} %get-tuple-element.10), kind=kLoop, calls=%fused_computation.4 | loop fusion | flops 524288 | bytes 3145728 | tf_op jit(solution)/shard_map/convert_element_type | solution.py:448
  130.1 0.0 copy-start
  130.1 0.0 copy-start.1
  130.1 1.3 copy.18
  131.4 0.3 copy.17
  131.8 0.0 copy-done
  131.8 0.0 copy-done.1
  131.8 0.0 copy-start.2
  131.8 0.0 copy-start.3
  131.8 1.3 fusion.1
  133.1 0.0 copy-done.2
  133.1 0.8 copy.21
  133.9 0.0 copy-done.3
  133.9 0.7 copy.22
Async XLA Ops:
  130.1 1.7 %copy-start = (bf16[256,1024]{1,0:T(8,128)(2,1)S(1)}, bf16[256,1024]{1,0:T(8,128)(2,1)}, u32[]{:S(2)}) copy-start(bf16[256,1024]{1,0:T(8,128)(2,1)} %in_gate.1) | copy-start | bytes 1572868
  130.1 1.7 %copy-start.1 = (bf16[256,1024]{1,0:T(8,128)(2,1)S(1)}, bf16[256,1024]{1,0:T(8,128)(2,1)}, u32[]{:S(2)}) copy-start(bf16[256,1024]{1,0:T(8,128)(2,1)} %values.1) | copy-start | bytes 1572868
  131.8 1.3 copy-start.2
  131.8 2.1 %copy-start.3 = (f32[64,1024]{1,0:T(8,128)S(1)}, f32[64,1024]{1,0:T(8,128)}, u32[]{:S(2)}) copy-start(f32[64,1024]{1,0:T(8,128)} %get-tuple-element.12) | copy-start | bytes 786436

commit v3 on v2

v3 whole, which is shorter than its diff:
```python
import functools

import jax
import jax.numpy as jnp
import numpy as np
from jax import lax
from jax.experimental import pallas as pl
from jax.experimental.pallas import tpu as pltpu
from jax.sharding import PartitionSpec as P

MESH = pl.DeviceIdType.MESH
F32 = jnp.float32
BF16 = jnp.bfloat16

RANKS = 64
POS = 256
CHAN = 16
GROUP = CHAN // 2
WIDTH = RANKS * CHAN
MODEL = 4096
VMEM_LIMIT = 60 * 2**20


def coords():
    i = lax.axis_index("ctx")
    return i // 16, (i // 4) % 4, (i // 2) % 2, i % 2


def device(x, y, z, b):
    return (((x * 4 + y) * 2 + z) * 2 + b, lax.axis_index("ch"))


def split(x):
    hi = x.astype(BF16)
    return hi, (x - hi.astype(F32)).astype(BF16)


def tables():
    n = RANKS * POS
    k1 = np.arange(RANKS) + 0.25
    first = 2 * np.pi * k1[:, None] * np.arange(RANKS)[None, :] / RANKS
    turn = 2 * np.pi * k1[:, None] * np.arange(POS)[None, :] / n
    second = 2 * np.pi * ((np.arange(POS)[:, None] * np.arange(POS)[None, :]) % POS) / POS

    def parts(table):
        hi = table.astype(jnp.bfloat16)
        lo = (table - hi.astype(np.float64)).astype(jnp.bfloat16)
        return hi, lo

    one = np.concatenate([np.cos(first), -np.sin(first)], 0)
    one_hi, one_lo = parts(one)
    cos, sin = np.cos(second), np.sin(second)
    two_hi, two_lo = parts(np.block([[cos, -sin], [sin, cos]]))
    last = np.concatenate([np.cos(first), np.sin(first)], 0).T / n
    last_hi, last_lo = parts(last)
    return (
        np.concatenate([one_hi, one_lo], 1),
        np.cos(turn).astype(np.float32),
        (-np.sin(turn)).astype(np.float32),
        two_hi,
        two_lo,
        np.concatenate([last_hi, last_lo, last_hi], 1),
    )


def wide(rows, i):
    return jnp.concatenate([rows[u, pl.ds(i, RANKS, stride=CHAN), :] for u in range(2)], 1)


def narrow(rows, i):
    return jnp.concatenate([rows[pl.ds(u * GROUP + i, RANKS, stride=CHAN), :] for u in range(2)], 1)


def put_wide(rows, i, signal):
    for u in range(2):
        rows[u, pl.ds(i, RANKS, stride=CHAN), :] = signal[:, u * 128 : (u + 1) * 128]


def put_narrow(rows, i, signal):
    for u in range(2):
        rows[pl.ds(u * GROUP + i, RANKS, stride=CHAN), :] = signal[:, u * 128 : (u + 1) * 128]


def turn(re, im, tabs, z_hi, z_lo, i):
    at = slice(i * RANKS, (i + 1) * RANKS)
    cos_t, sin_t = tabs[1][...], tabs[2][...]
    z_hi[at, :POS], z_lo[at, :POS] = split(re * cos_t - im * sin_t)
    z_hi[at, POS:], z_lo[at, POS:] = split(re * sin_t + im * cos_t)


def transform(pick, rows, count, tabs, z_hi, z_lo, spec):
    for i in range(count):
        x = pick(rows, i).astype(BF16)
        a = jnp.dot(tabs[0][...], jnp.concatenate([x, x], 0), preferred_element_type=F32)
        turn(a[:RANKS], a[RANKS:], tabs, z_hi, z_lo, i)
    second(count, tabs, z_hi, z_lo, spec)


def second(count, tabs, z_hi, z_lo, spec):
    _, _, _, two_hi, two_lo, _ = tabs

    def block(i, carry):
        at = pl.ds(pl.multiple_of(i * 256, 256), 256)
        spec[at, :] = (
            jnp.dot(z_hi[at, :], two_hi[...], preferred_element_type=F32)
            + jnp.dot(z_hi[at, :], two_lo[...], preferred_element_type=F32)
            + jnp.dot(z_lo[at, :], two_hi[...], preferred_element_type=F32)
        )
        return carry

    lax.fori_loop(0, count * RANKS // 256, block, 0)


def signals_of(put, rows, count, tabs, z_hi, z_lo, spec):
    second(count, tabs, z_hi, z_lo, spec)
    cos_t, sin_t, last = tabs[1], tabs[2], tabs[5]
    for i in range(count):
        at = slice(i * RANKS, (i + 1) * RANKS)
        re, im = spec[at, :POS], spec[at, POS:]
        hi_re, lo_re = split(re * cos_t[...] - im * sin_t[...])
        hi_im, lo_im = split(re * sin_t[...] + im * cos_t[...])
        stack = jnp.concatenate([hi_re, hi_im, hi_re, hi_im, lo_re, lo_im], 0)
        put(rows, i, jnp.dot(last[...], stack, preferred_element_type=F32))


def spectral_product(left, left_row, right, right_row, conj_right, z_hi, z_lo, row):
    def block(i, carry):
        def at(start):
            return pl.ds(pl.multiple_of(start + i * 64, 64), 64)

        one, two, out = at(left_row), at(right_row), at(row)
        a, b, c, d = left[one, :POS], left[one, POS:], right[two, :POS], right[two, POS:]
        if conj_right:
            re, im = a * c + b * d, b * c - a * d
        else:
            re, im = a * c - b * d, -(a * d + b * c)
        z_hi[out, :POS], z_lo[out, :POS] = split(re)
        z_hi[out, POS:], z_lo[out, POS:] = split(im)
        return carry

    lax.fori_loop(0, GROUP, block, 0)


def load_wide(blocks, g, rows):
    for s in range(RANKS):
        for u in range(2):
            rows[u, s * CHAN : (s + 1) * CHAN, :] = blocks[s, g, :, u * 128 : (u + 1) * 128].astype(F32)


def store_wide(rows, blocks, g):
    for s in range(RANKS):
        for u in range(2):
            blocks[s, g, :, u * 128 : (u + 1) * 128] = rows[u, s * CHAN : (s + 1) * CHAN, :].astype(BF16)


def load_narrow(blocks, g, rows):
    for s in range(RANKS):
        rows[s * CHAN : (s + 1) * CHAN, :] = blocks[s, g].astype(F32)


def store_narrow(rows, blocks, g):
    for s in range(RANKS):
        blocks[s, g] = rows[s * CHAN : (s + 1) * CHAN, :].astype(BF16)


def partner(e):
    x, y, z, b = coords()
    return device((x + e // 16) % 4, (y + (e // 4) % 4) % 4, (z + (e // 2) % 2) % 2, (b + e % 2) % 2)


def remote(src, dst, there, send_sem, recv_sem):
    return pltpu.make_async_remote_copy(
        src_ref=src, dst_ref=dst, send_sem=send_sem, recv_sem=recv_sem, device_id=there, device_id_type=MESH
    )


def start_exchange(src, got, g, send_sem, recv_sem):
    me = lax.axis_index("ctx")

    def send(e):
        there = partner(e)
        remote(src.at[there[0], g], got.at[me, g], there, send_sem, recv_sem).start()

    def far(i, carry):
        send((i // 2) * 4 + i % 2 + 2)
        return carry

    def near(i, carry):
        send((i // 2) * 4 + i % 2)
        return carry

    lax.fori_loop(0, 32, far, 0)
    lax.fori_loop(1, 32, near, 0)
    got[me, g] = src[me, g]


def finish(blocks, g, sem):
    others = blocks.at[pl.ds(0, RANKS - 1), g]
    pltpu.make_async_copy(others, others, sem).wait()


def kernel(
    *refs,
):
    far_refs, (
        out_gate_grad, got_out, weight_grad,
        src_in, got_in, src_out, src_c, got_c, src_d, got_d,
        weights, turned, planes, pair_grad, grad_y,
        rows, short_rows, z_hi, z_lo, spec, spec_0, spec_1, spec_d, product_sum,
        pair_mixed, send_one, recv_hop, recv_one, send_two, recv_two, send_three, recv_three, own,
        ex_send, ex_recv, ag_send, ag_recv, sib_send, sib_recv, rs_send, rs_recv,
        stage_sem, *held_refs,
    ) = refs[:OPERANDS], refs[OPERANDS:]
    staging = [
        pltpu.make_async_copy(source, target, stage_sem.at[n])
        for n, (source, target) in enumerate(zip(far_refs, held_refs))
    ]
    in_gate, values, taps, shard, out_grad, out_gate, one, cos_t, sin_t, two_hi, two_lo, last = held_refs
    for copy in staging:
        copy.start()
    x, y, z, b = coords()
    sibling = device(x, y, z, 1 - b)
    tabs = (one, cos_t, sin_t, two_hi, two_lo, last)
    half = WIDTH // 2
    halves = (pl.ds(0, half), pl.ds(half, half))
    sent = []

    barrier = pltpu.get_barrier_semaphore()

    def say(e, carry):
        pl.semaphore_signal(barrier, inc=1, device_id=partner(e), device_id_type=MESH)
        return carry

    lax.fori_loop(1, RANKS, say, 0)
    for copy in staging[:4]:
        copy.wait()
    weights[x, y, z, b] = shard[...]
    for n in range(WIDTH // 128):
        at = slice(n * 128, (n + 1) * 128)
        gated = (in_gate[:, at].astype(F32) * values[:, at].astype(F32)).astype(BF16).astype(F32)
        both = (gated.T.reshape(8, CHAN, POS), taps[:, at].astype(F32).T.reshape(8, CHAN, POS))
        for g in range(2):
            kept = slice(g * GROUP, (g + 1) * GROUP)
            src_in[n * 8 : (n + 1) * 8, g] = jnp.concatenate([a[:, kept] for a in both], 1).astype(BF16)
    pl.semaphore_wait(barrier, RANKS - 1)

    def gather(slot, n, there):
        copy = remote(slot, slot, there, ag_send.at[n], ag_recv.at[n])
        copy.start()
        sent.append(copy)
        return copy

    relays = []

    def relay(slot):
        n = len(relays)
        copy = remote(slot, slot, sibling, sib_send.at[n], sib_recv.at[n])
        copy.start()
        sent.append(copy)
        relays.append(copy)

    def first_round(plane, n):
        stage = []
        for d in (2, 1, 3):
            stage.append(gather(weights.at[x, y, plane, b, :, halves[0]], n + d, device((x + d) % 4, y, z, b)))
            stage.append(gather(weights.at[x, y, plane, b, :, halves[1]], n + 3 + d, device(x, (y + d) % 4, z, b)))
        relay(weights.at[x, y, plane, b])
        return stage

    def second_round(plane, n, stage):
        for copy in stage:
            copy.wait_recv()
        stage = []
        for d in (1, 3):
            stage.append(gather(weights.at[:, y, plane, b, :, halves[0]], n + d, device(x, (y + d) % 4, z, b)))
            stage.append(gather(weights.at[x, :, plane, b, :, halves[1]], n + 3 + d, device((x + d) % 4, y, z, b)))
        for d in (2, 1, 3):
            relay(weights.at[(x + 4 - d) % 4, y, plane, b, :, halves[0]])
            relay(weights.at[x, (y + 4 - d) % 4, plane, b, :, halves[1]])
        return stage

    def pass_on(plane, n, stage):
        onward = []
        for i, (d, part) in enumerate(((1, pl.ds(0, 32)), (3, pl.ds(32, 32)))):
            stage[2 * i].wait_recv()
            at = (y + 4 - d) % 4
            slot = weights.at[:, at, plane, b, part, halves[0]]
            onward.append(gather(slot, n + 2 * i, device(x, (y + d) % 4, z, b)))
            relay(weights.at[:, at, plane, b, :, halves[0]])
            stage[2 * i + 1].wait_recv()
            at = (x + 4 - d) % 4
            slot = weights.at[at, :, plane, b, part, halves[1]]
            onward.append(gather(slot, n + 2 * i + 1, device((x + d) % 4, y, z, b)))
            relay(weights.at[at, :, plane, b, :, halves[1]])
        return onward

    def last_round(plane, onward):
        for copy in onward:
            copy.wait_recv()
        relay(weights.at[:, (y + 2) % 4, plane, b, :, halves[0]])
        relay(weights.at[(x + 2) % 4, :, plane, b, :, halves[1]])

    far = gather(weights.at[x, y, z, b], 0, device(x, y, 1 - z, b))
    near_stage = first_round(z, 0)
    for g in range(2):
        start_exchange(src_in, got_in, g, ex_send.at[g], ex_recv.at[g])
    far.wait_recv()
    far_stage = first_round(1 - z, 6)

    for copy in staging[4:]:
        copy.wait()
    for n in range(MODEL // 128):
        at = slice(n * 128, (n + 1) * 128)
        turned[at, :] = out_grad[:, at].astype(F32).T.astype(BF16)

    near_stage = second_round(z, 12, near_stage)
    for n in range(16):
        for p in range(2):
            planes[p, :, n * 128 : (n + 1) * 128] = out_grad[:, n * 256 + p * 128 : n * 256 + (p + 1) * 128]

    def mine(n, carry):
        at = pl.ds(pl.multiple_of(n * 128 + b * 64, 64), 64)
        pair_grad[b, pl.ds(pl.multiple_of(n * 64, 64), 64), :] = turned[at, :]
        return carry

    def theirs(n, carry):
        at = pl.ds(pl.multiple_of(n * 128 + (1 - b) * 64, 64), 64)
        kept = pl.ds(pl.multiple_of(n * 64, 64), 64)
        turned[kept, :] = turned[at, :]
        return carry

    lax.fori_loop(0, MODEL // 128, mine, 0)
    lax.fori_loop(0, MODEL // 128, theirs, 0)
    pair = remote(turned.at[pl.ds(0, MODEL // 2)], pair_grad.at[b], sibling, rs_send.at[20], rs_recv.at[20])
    pair.start()
    sent.append(pair)

    far_stage = second_round(1 - z, 18, far_stage)

    specs = (spec_0, spec_1)
    onward = []
    for g, (plane, n, stage) in enumerate(((z, 25, near_stage), (1 - z, 29, far_stage))):
        finish(got_in, g, ex_recv.at[g])
        load_wide(got_in, g, rows)
        if g == 1:
            onward.append(pass_on(plane, n, stage))
        transform(wide, rows, CHAN, tabs, z_hi, z_lo, specs[g])
        if g == 0:
            onward.append(pass_on(plane, n, stage))
        spectral_product(specs[g], 0, specs[g], WIDTH // 2, False, z_hi, z_lo, 0)
        signals_of(put_narrow, short_rows, GROUP, tabs, z_hi, z_lo, spec)
        store_narrow(short_rows, src_c, g)
        start_exchange(src_c, got_c, g, ex_send.at[2 + g], ex_recv.at[2 + g])
    near_onward, far_onward = onward

    def share(plane, at):
        right = weights[:, :, plane, :, :, at].reshape(MODEL // 2, 256)
        return jnp.dot(planes[plane], right, preferred_element_type=F32)

    last_round(z, near_onward)
    last_round(1 - z, far_onward)
    near_relays = relays[:1] + relays[2:8] + relays[14:18] + relays[22:24]
    far_relays = relays[1:2] + relays[8:14] + relays[18:22] + relays[24:26]
    for copy in near_relays:
        copy.wait_recv()
    for n in range(WIDTH // 256):
        at = slice(n * 256, (n + 1) * 256)
        product_sum[:, at] = share(z, at)
    for copy in far_relays:
        copy.wait_recv()
    for n in range(WIDTH // 256):
        at = slice(n * 256, (n + 1) * 256)
        product = (product_sum[:, at] + share(1 - z, at)).astype(BF16)
        grad_y[:, at] = product
        grad_conv = (product.astype(F32) * out_gate[:, at].astype(F32)).astype(BF16).astype(F32)
        grad_conv = grad_conv.T.reshape(16, CHAN, POS)
        for g in range(2):
            kept = grad_conv[:, g * GROUP : (g + 1) * GROUP]
            pair_of = jnp.concatenate([kept[:, :, :128], kept[:, :, 128:]], 1)
            src_d[n * 16 : (n + 1) * 16, g] = pair_of.astype(BF16)
    for g in range(2):
        start_exchange(src_d, got_d, g, ex_send.at[4 + g], ex_recv.at[4 + g])

    for g in range(2):
        finish(got_c, g, ex_recv.at[2 + g])
    for n in range(WIDTH // 128):
        at = slice(n * 128, (n + 1) * 128)
        block = got_c[n * 8 : (n + 1) * 8].astype(F32)
        for u in range(2):
            there = slice(u * 128, (u + 1) * 128)
            conv = block[:, :, u * GROUP : (u + 1) * GROUP].reshape(128, 128).T
            pair_mixed[b, there, at] = (out_gate[there, at].astype(F32) * conv).astype(BF16)
            out_gate_grad[there, at] = (grad_y[there, at].astype(F32) * conv).astype(BF16)
    mixed = remote(pair_mixed.at[b], pair_mixed.at[b], sibling, rs_send.at[0], rs_recv.at[0])
    mixed.start()
    sent.append(mixed)

    def partial(first_row, count, at):
        at_rows = pl.ds(pl.multiple_of(first_row, 128), count)
        left = jnp.concatenate([pair_grad[0, at_rows, :], pair_grad[1, at_rows, :]], 1)
        return jnp.dot(left, pair_mixed[:, :, at].reshape(2 * POS, half), preferred_element_type=F32)

    def reduce_to(src, dst, n, there):
        copy = remote(src, dst, there, rs_send.at[n], rs_recv.at[n])
        copy.start()
        sent.append(copy)
        return copy

    pair.wait_recv()
    mixed.wait_recv()
    lanes = (slice(0, half), slice(half, WIDTH))

    def chunk(h, to, part):
        if h == 0:
            return partial(to * 512 + part * 256, 256, lanes[0])
        two = [partial((2 * part + u) * 512 + to * 128, 128, lanes[1]) for u in range(2)]
        return jnp.concatenate(two, 0)

    def along(h, d):
        return device((x + d) % 4, y, z, b) if h == 0 else device(x, (y + d) % 4, z, b)

    parts = (slice(0, 256), slice(256, 512))
    place = (x, y)
    hops, stage = [], []
    for h in range(2):
        for i, d in enumerate((1, 3)):
            send_one[h, 2, parts[i], :] = chunk(h, (place[h] + 2) % 4, i).astype(BF16)
            hops.append(
                reduce_to(send_one.at[h, 2, pl.ds(i * 256, 256)], recv_hop.at[h, i], 1 + 6 * h + i, along(h, d))
            )
    for h in range(2):
        for i, d in enumerate((1, 3)):
            j = 1 - i
            send_one[h, i, parts[j], :] = chunk(h, (place[h] + d) % 4, j).astype(BF16)
            rows_j = pl.ds(j * 256, 256)
            stage.append(
                reduce_to(send_one.at[h, i, rows_j], recv_one.at[h, i, rows_j], 3 + 6 * h + i, along(h, d))
            )
    for g in range(2):
        finish(got_d, g, ex_recv.at[4 + g])
        load_narrow(got_d, g, short_rows)
        transform(narrow, short_rows, GROUP, tabs, z_hi, z_lo, spec_d)
        spectral_product(specs[g], WIDTH // 2, spec_d, 0, True, z_hi, z_lo, 0)
        spectral_product(specs[g], 0, spec_d, 0, True, z_hi, z_lo, WIDTH // 2)
        signals_of(put_wide, rows, CHAN, tabs, z_hi, z_lo, spec)
        store_wide(rows, src_out, g)
        start_exchange(src_out, got_out, g, ex_send.at[6 + g], ex_recv.at[6 + g])
        if g == 1:
            break
        for h in range(2):
            for i, d in enumerate((1, 3)):
                mine = chunk(h, (place[h] + d) % 4, i)
                hops[2 * h + i].wait_recv()
                send_one[h, i, parts[i], :] = (mine + recv_hop[h, i].astype(F32)).astype(BF16)
                rows_i = pl.ds(i * 256, 256)
                stage.append(
                    reduce_to(send_one.at[h, i, rows_i], recv_one.at[h, i, rows_i], 5 + 6 * h + i, along(h, d))
                )
        for h in range(2):
            for i in range(2):
                own[h, parts[i], :] = chunk(h, place[h], i)
    for copy in stage:
        copy.wait_recv()

    def summed(h, place):
        at = pl.ds(pl.multiple_of(place * 128, 128), 128)
        total = own[h, at, :]
        for d in range(2):
            total = total + recv_one[h, d, at, :].astype(F32)
        return total

    stage = []
    for d in (2, 1, 3):
        to = (y + d) % 4
        send_two[0, d - 1] = summed(0, to).astype(BF16)
        stage.append(reduce_to(send_two.at[0, d - 1], recv_two.at[0, d - 1], 12 + d, device(x, to, z, b)))
        to = (x + d) % 4
        send_two[1, d - 1] = summed(1, to).astype(BF16)
        stage.append(reduce_to(send_two.at[1, d - 1], recv_two.at[1, d - 1], 15 + d, device(to, y, z, b)))
    own[0, 0:128, :] = summed(0, y)
    own[1, 0:128, :] = summed(1, x)
    for copy in stage:
        copy.wait_recv()
    for h in range(2):
        total = own[h, 0:128, :]
        for d in range(3):
            total = total + recv_two[h, d].astype(F32)
        own[h, 0:128, :] = total
    there = pl.ds(pl.multiple_of((1 - z) * 64, 64), 64)
    here = pl.ds(pl.multiple_of(z * 64, 64), 64)
    send_three[0] = own[0, there, :].astype(BF16)
    send_three[1] = own[1, there, :].astype(BF16)
    reduce_to(send_three, recv_three, 19, device(x, y, 1 - z, b)).wait_recv()
    for h in range(2):
        weight_grad[:, lanes[h]] = own[h, here, :] + recv_three[h].astype(F32)

    for g in range(2):
        finish(got_out, g, ex_recv.at[6 + g])
    for n, blocks in enumerate((src_in, src_c, src_d, src_out)):
        for g in range(2):
            finish(blocks, g, ex_send.at[2 * n + g])
    for copy in sent:
        copy.wait_send()


def last_products(
    blocks, in_gate, values, out_gate_in, weight_in, out_gate_grad, in_gate_grad, values_grad, taps_grad, weight_grad
):
    for n in range(2):
        at = slice(n * 128, (n + 1) * 128)
        block = blocks[n * 8 : (n + 1) * 8].astype(F32)
        grad_gated = block[:, :, :GROUP].reshape(128, POS).T
        in_gate_grad[:, at] = (grad_gated * values[:, at].astype(F32)).astype(BF16)
        values_grad[:, at] = (grad_gated * in_gate[:, at].astype(F32)).astype(BF16)
        taps_grad[:, at] = block[:, :, GROUP:].reshape(128, POS).T
    out_gate_grad[...] = out_gate_in[...]
    weight_grad[...] = weight_in[...]


OPERANDS = 12
WHOLE = pl.BlockSpec(memory_space=pltpu.VMEM)
DMA = pltpu.SemaphoreType.DMA


def on_device(out_gate, in_gate, values, filter_taps, out_grad, out_weight):
    tabs = [jnp.asarray(table) for table in tables()]
    shape = jax.ShapeDtypeStruct
    half = WIDTH // 2
    operands = (in_gate, values, filter_taps, out_weight.T, out_grad, out_gate, *tabs)
    outs = [shape((POS, WIDTH), BF16), shape((RANKS, 2, CHAN, POS), BF16), shape((64, WIDTH), F32)]
    out_gate_grad, got_out, weight_grad = pl.pallas_call(
        kernel,
        name="hyena_backward",
        out_shape=outs,
        in_specs=[pl.BlockSpec(memory_space=pl.ANY)] * len(operands),
        out_specs=[WHOLE] * len(outs),
        scratch_shapes=[pltpu.VMEM((RANKS, 2, CHAN, POS), BF16) for _ in range(3)]
        + [pltpu.VMEM((RANKS, 2, CHAN, 128), BF16) for _ in range(4)]
        + [
            pltpu.VMEM((4, 4, 2, 2, 64, WIDTH), BF16),
            pltpu.VMEM((MODEL, POS), BF16),
            pltpu.VMEM((2, POS, MODEL // 2), BF16),
            pltpu.VMEM((2, MODEL // 2, POS), BF16),
            pltpu.VMEM((POS, WIDTH), BF16),
            pltpu.VMEM((2, WIDTH, 128), F32),
            pltpu.VMEM((WIDTH, 128), F32),
            pltpu.VMEM((WIDTH, 2 * POS), BF16),
            pltpu.VMEM((WIDTH, 2 * POS), BF16),
            pltpu.VMEM((WIDTH, 2 * POS), F32),
            pltpu.VMEM((WIDTH, 2 * POS), F32),
            pltpu.VMEM((WIDTH, 2 * POS), F32),
            pltpu.VMEM((WIDTH // 2, 2 * POS), F32),
            pltpu.VMEM((POS, WIDTH), F32),
            pltpu.VMEM((2, POS, WIDTH), BF16),
            pltpu.VMEM((2, 3, 512, half), BF16),
            pltpu.VMEM((2, 2, 256, half), BF16),
            pltpu.VMEM((2, 2, 512, half), BF16),
            pltpu.VMEM((2, 3, 128, half), BF16),
            pltpu.VMEM((2, 3, 128, half), BF16),
            pltpu.VMEM((2, 64, half), BF16),
            pltpu.VMEM((2, 64, half), BF16),
            pltpu.VMEM((2, 512, half), F32),
            DMA((8,)),
            DMA((8,)),
            DMA((33,)),
            DMA((33,)),
            DMA((26,)),
            DMA((26,)),
            DMA((21,)),
            DMA((21,)),
            DMA((OPERANDS,)),
        ]
        + [pltpu.VMEM(a.shape, a.dtype) for a in operands],
        compiler_params=pltpu.CompilerParams(
            collective_id=0, has_side_effects=True, vmem_limit_bytes=VMEM_LIMIT
        ),
    )(*operands)
    wide_block = pl.BlockSpec((POS, 256), lambda n: (0, n))
    *grads, weight_grad = pl.pallas_call(
        last_products,
        name="last_products",
        grid=(WIDTH // 256,),
        out_shape=[shape((POS, WIDTH), BF16)] * 3 + [shape((POS, WIDTH), F32), shape((64, WIDTH), F32)],
        in_specs=[
            pl.BlockSpec((16, 2, CHAN, POS), lambda n: (n, 0, 0, 0)),
            wide_block,
            wide_block,
            wide_block,
            pl.BlockSpec((64, 256), lambda n: (0, n)),
        ],
        out_specs=[wide_block] * 4 + [pl.BlockSpec((64, 256), lambda n: (0, n))],
    )(got_out, in_gate, values, out_gate_grad, weight_grad)
    return (*grads, weight_grad.T)


def solution(mesh):
    return jax.shard_map(
        on_device,
        mesh=mesh,
        in_specs=(
            P("ctx", "ch"),
            P("ctx", "ch"),
            P("ctx", "ch"),
            P("ctx", "ch"),
            P("ctx", None),
            P("ch", "ctx"),
        ),
        out_specs=(P("ctx", "ch"), P("ctx", "ch"), P("ctx", "ch"), P("ctx", "ch"), P("ch", "ctx")),
        check_vma=False,
    )
```

time: 135 us -> 123 us (0.911)
  Pallas kernels: 128 us -> 122 us
  local copies, waits for them, and re-layouts: 3.15 us -> 0 us
  other arithmetic: 2.63 us -> 0 us
    pallas_call x1 -> x2, Pallas kernels: 128 us -> 122 us  [the longest x1 117 us: on_device(): pl.pallas_call(kernel, name='hyena_backward', out_shape=outs, in_specs=[p...]
    convert_element_type x2 -> x0, other arithmetic: 2.63 us -> none  [the longest x1 1.36 us: on_device(): taps_grad = got_tg.reshape(WIDTH, POS).T.astype(F32)]
    convert_element_type x2 -> x0, local copies, waits for them, and re-layouts: 1.64 us -> none  [the longest x1 1.31 us: on_device(): taps_grad = got_tg.reshape(WIDTH, POS).T.astype(F32)]
    unnamed x10 -> x0, local copies, waits for them, and re-layouts: 1.52 us -> none
where the time goes in v3:
time: 123 us; the launch traced here: 122 us
  Pallas kernels  122 us (99%)
    pallas_call x1, Pallas kernels, on_device(): pl.pallas_call(kernel, name='hyena_backward', out_shape=outs, in_specs=[p...  117 us
    pallas_call x1, Pallas kernels, on_device(): pl.pallas_call(last_products, name='last_products', grid=(WIDTH // 256,),...  4.17 us

profile of v3, /device:TPU:64, one launch (start us, length us, event | category | flops | bytes accessed | tf_op | source)
XLA Modules:
  0.0 122.3 jit_solution(2461429582548140919)
XLA Ops:
  0.6 117.4 %hyena_backward.1 = (bf16[256,1024]{1,0:T(8,128)(2,1)}, bf16[64,2,16,256]{3,2,1,0:T(8,128)(2,1)}, f32[64,1024]{1,0:T(8,128)}) custom-call(bf16[256,1024]{1,0:T(8,128)(2,1)} %in_gate.1, bf16[256,1024]{1,0:T(8,128)(2,1)} %values.1, bf16[256,1024]{1,0:T(8,128)(2,1)} %refs_2_.1, bf16[64,1024]{1,0:T(8,128)(2,1)} %bitcast.2, bf16[256,4096]{1,0:T(8,128)(2,1)} %refs_4_.1, ...), custom_call_target="tpu_custom_call" | custom-call | tf_op jit(solution)/shard_map/hyena_backward/pallas_call | solution.py:531
  118.0 4.2 %last_products.1 = (bf16[256,1024]{1,0:T(8,128)(2,1)}, bf16[256,1024]{1,0:T(8,128)(2,1)}, bf16[256,1024]{1,0:T(8,128)(2,1)}, f32[256,1024]{1,0:T(8,128)}, f32[64,1024]{1,0:T(8,128)}) custom-call(bf16[64,2,16,256]{3,2,1,0:T(8,128)(2,1)} %get-tuple-element.13.blocks, bf16[256,1024]{1,0:T(8,128)(2,1)} %in_gate.1, bf16[256,1024]{1,0:T(8,128)(2,1)} %values.1, ...), custom_call_target="tpu_custom_call" | custom-call | tf_op jit(solution)/shard_map/last_products/pallas_call | solution.py:579

commit v4 on v3

--- a/solution.py
+++ b/solution.py
@@ -101,18 +101,19 @@
 
     def block(i, carry):
         at = pl.ds(pl.multiple_of(i * 256, 256), 256)
-        spec[at, :] = (
-            jnp.dot(z_hi[at, :], two_hi[...], preferred_element_type=F32)
-            + jnp.dot(z_hi[at, :], two_lo[...], preferred_element_type=F32)
-            + jnp.dot(z_lo[at, :], two_hi[...], preferred_element_type=F32)
+        total = jnp.dot(z_hi[at, :], two_hi[...], preferred_element_type=F32) + jnp.dot(
+            z_hi[at, :], two_lo[...], preferred_element_type=F32
         )
+        if z_lo is not None:
+            total = total + jnp.dot(z_lo[at, :], two_hi[...], preferred_element_type=F32)
+        spec[at, :] = total
         return carry
 
     lax.fori_loop(0, count * RANKS // 256, block, 0)
 
 
-def signals_of(put, rows, count, tabs, z_hi, z_lo, spec):
-    second(count, tabs, z_hi, z_lo, spec)
+def signals_of(put, rows, count, tabs, z_hi, spec):
+    second(count, tabs, z_hi, None, spec)
     cos_t, sin_t, last = tabs[1], tabs[2], tabs[5]
     for i in range(count):
         at = slice(i * RANKS, (i + 1) * RANKS)
@@ -123,7 +124,7 @@
         put(rows, i, jnp.dot(last[...], stack, preferred_element_type=F32))
 
 
-def spectral_product(left, left_row, right, right_row, conj_right, z_hi, z_lo, row):
+def spectral_product(left, left_row, right, right_row, conj_right, z, row):
     def block(i, carry):
         def at(start):
             return pl.ds(pl.multiple_of(start + i * 64, 64), 64)
@@ -134,8 +135,8 @@
             re, im = a * c + b * d, b * c - a * d
         else:
             re, im = a * c - b * d, -(a * d + b * c)
-        z_hi[out, :POS], z_lo[out, :POS] = split(re)
-        z_hi[out, POS:], z_lo[out, POS:] = split(im)
+        z[out, :POS] = re.astype(BF16)
+        z[out, POS:] = im.astype(BF16)
         return carry
 
     lax.fori_loop(0, GROUP, block, 0)
@@ -164,8 +165,7 @@
 
 
 def partner(e):
-    x, y, z, b = coords()
-    return device((x + e // 16) % 4, (y + (e // 4) % 4) % 4, (z + (e // 2) % 2) % 2, (b + e % 2) % 2)
+    return (lax.rem(lax.axis_index("ctx") + e, RANKS), lax.axis_index("ch"))
 
 
 def remote(src, dst, there, send_sem, recv_sem):
@@ -181,16 +181,13 @@
         there = partner(e)
         remote(src.at[there[0], g], got.at[me, g], there, send_sem, recv_sem).start()
 
-    def far(i, carry):
-        send((i // 2) * 4 + i % 2 + 2)
-        return carry
-
-    def near(i, carry):
-        send((i // 2) * 4 + i % 2)
-        return carry
-
-    lax.fori_loop(0, 32, far, 0)
-    lax.fori_loop(1, 32, near, 0)
+    for r in (2, 1, 3, 0):
+
+        def group(i, carry):
+            send(4 * i + r)
+            return carry
+
+        lax.fori_loop(1 if r == 0 else 0, RANKS // 4, group, 0, unroll=True)
     got[me, g] = src[me, g]
 
 
@@ -231,7 +228,7 @@
         pl.semaphore_signal(barrier, inc=1, device_id=partner(e), device_id_type=MESH)
         return carry
 
-    lax.fori_loop(1, RANKS, say, 0)
+    lax.fori_loop(1, RANKS, say, 0, unroll=9)
     for copy in staging[:4]:
         copy.wait()
     weights[x, y, z, b] = shard[...]
@@ -347,8 +344,8 @@
         transform(wide, rows, CHAN, tabs, z_hi, z_lo, specs[g])
         if g == 0:
             onward.append(pass_on(plane, n, stage))
-        spectral_product(specs[g], 0, specs[g], WIDTH // 2, False, z_hi, z_lo, 0)
-        signals_of(put_narrow, short_rows, GROUP, tabs, z_hi, z_lo, spec)
+        spectral_product(specs[g], 0, specs[g], WIDTH // 2, False, z_hi, 0)
+        signals_of(put_narrow, short_rows, GROUP, tabs, z_hi, spec)
         store_narrow(short_rows, src_c, g)
         start_exchange(src_c, got_c, g, ex_send.at[2 + g], ex_recv.at[2 + g])
     near_onward, far_onward = onward
@@ -358,15 +355,14 @@
         return jnp.dot(planes[plane], right, preferred_element_type=F32)
 
     last_round(z, near_onward)
-    last_round(1 - z, far_onward)
     near_relays = relays[:1] + relays[2:8] + relays[14:18] + relays[22:24]
-    far_relays = relays[1:2] + relays[8:14] + relays[18:22] + relays[24:26]
     for copy in near_relays:
         copy.wait_recv()
     for n in range(WIDTH // 256):
         at = slice(n * 256, (n + 1) * 256)
         product_sum[:, at] = share(z, at)
-    for copy in far_relays:
+    last_round(1 - z, far_onward)
+    for copy in relays[1:2] + relays[8:14] + relays[18:22] + relays[24:26]:
         copy.wait_recv()
     for n in range(WIDTH // 256):
         at = slice(n * 256, (n + 1) * 256)
@@ -440,9 +436,9 @@
         finish(got_d, g, ex_recv.at[4 + g])
         load_narrow(got_d, g, short_rows)
         transform(narrow, short_rows, GROUP, tabs, z_hi, z_lo, spec_d)
-        spectral_product(specs[g], WIDTH // 2, spec_d, 0, True, z_hi, z_lo, 0)
-        spectral_product(specs[g], 0, spec_d, 0, True, z_hi, z_lo, WIDTH // 2)
-        signals_of(put_wide, rows, CHAN, tabs, z_hi, z_lo, spec)
+        spectral_product(specs[g], WIDTH // 2, spec_d, 0, True, z_hi, 0)
+        spectral_product(specs[g], 0, spec_d, 0, True, z_hi, WIDTH // 2)
+        signals_of(put_wide, rows, CHAN, tabs, z_hi, spec)
         store_wide(rows, src_out, g)
         start_exchange(src_out, got_out, g, ex_send.at[6 + g], ex_recv.at[6 + g])
         if g == 1:

time: 123 us -> 119 us (0.967)
  Pallas kernels: 122 us -> 118 us
    pallas_call x1, Pallas kernels: 117 us -> 114 us  [on_device(): pl.pallas_call(kernel, name='hyena_backward', out_shape=outs, in_specs=[p...]
where the time goes in v4:
time: 119 us
  Pallas kernels  118 us (99%)
    pallas_call x1, Pallas kernels, on_device(): pl.pallas_call(kernel, name='hyena_backward', out_shape=outs, in_specs=[p...  114 us
    pallas_call x1, Pallas kernels, on_device(): pl.pallas_call(last_products, name='last_products', grid=(WIDTH // 256,),...  4.17 us

profile of v4, /device:TPU:64, one launch (start us, length us, event | category | flops | bytes accessed | tf_op | source)
XLA Modules:
  0.0 119.1 jit_solution(13961197864212063879)
XLA Ops:
  0.6 114.1 %hyena_backward.1 = (bf16[256,1024]{1,0:T(8,128)(2,1)}, bf16[64,2,16,256]{3,2,1,0:T(8,128)(2,1)}, f32[64,1024]{1,0:T(8,128)}) custom-call(bf16[256,1024]{1,0:T(8,128)(2,1)} %in_gate.1, bf16[256,1024]{1,0:T(8,128)(2,1)} %values.1, bf16[256,1024]{1,0:T(8,128)(2,1)} %refs_2_.1, bf16[64,1024]{1,0:T(8,128)(2,1)} %bitcast.2, bf16[256,4096]{1,0:T(8,128)(2,1)} %refs_4_.1, ...), custom_call_target="tpu_custom_call" | custom-call | tf_op jit(solution)/shard_map/hyena_backward/pallas_call | solution.py:527
  114.8 4.2 %last_products.1 = (bf16[256,1024]{1,0:T(8,128)(2,1)}, bf16[256,1024]{1,0:T(8,128)(2,1)}, bf16[256,1024]{1,0:T(8,128)(2,1)}, f32[256,1024]{1,0:T(8,128)}, f32[64,1024]{1,0:T(8,128)}) custom-call(bf16[64,2,16,256]{3,2,1,0:T(8,128)(2,1)} %get-tuple-element.13.blocks, bf16[256,1024]{1,0:T(8,128)(2,1)} %in_gate.1, bf16[256,1024]{1,0:T(8,128)(2,1)} %values.1, ...), custom_call_target="tpu_custom_call" | custom-call | tf_op jit(solution)/shard_map/last_products/pallas_call | solution.py:575

commit v5 on v4

--- a/solution.py
+++ b/solution.py
@@ -379,17 +379,22 @@
 
     for g in range(2):
         finish(got_c, g, ex_recv.at[2 + g])
+
+    def conv_at(n, u):
+        block = got_c[n * 8 : (n + 1) * 8].astype(F32)
+        return block[:, :, u * GROUP : (u + 1) * GROUP].reshape(128, 128).T
+
+    mixed = []
     for n in range(WIDTH // 128):
         at = slice(n * 128, (n + 1) * 128)
-        block = got_c[n * 8 : (n + 1) * 8].astype(F32)
         for u in range(2):
             there = slice(u * 128, (u + 1) * 128)
-            conv = block[:, :, u * GROUP : (u + 1) * GROUP].reshape(128, 128).T
-            pair_mixed[b, there, at] = (out_gate[there, at].astype(F32) * conv).astype(BF16)
-            out_gate_grad[there, at] = (grad_y[there, at].astype(F32) * conv).astype(BF16)
-    mixed = remote(pair_mixed.at[b], pair_mixed.at[b], sibling, rs_send.at[0], rs_recv.at[0])
-    mixed.start()
-    sent.append(mixed)
+            pair_mixed[b, there, at] = (out_gate[there, at].astype(F32) * conv_at(n, u)).astype(BF16)
+        if n % 4 == 3:
+            part = pair_mixed.at[b, :, halves[n // 4]]
+            mixed.append(remote(part, part, sibling, rs_send.at[21 * (n // 4)], rs_recv.at[21 * (n // 4)]))
+            mixed[-1].start()
+    sent.extend(mixed)
 
     def partial(first_row, count, at):
         at_rows = pl.ds(pl.multiple_of(first_row, 128), count)
@@ -403,7 +408,6 @@
         return copy
 
     pair.wait_recv()
-    mixed.wait_recv()
     lanes = (slice(0, half), slice(half, WIDTH))
 
     def chunk(h, to, part):
@@ -419,6 +423,7 @@
     place = (x, y)
     hops, stage = [], []
     for h in range(2):
+        mixed[h].wait_recv()
         for i, d in enumerate((1, 3)):
             send_one[h, 2, parts[i], :] = chunk(h, (place[h] + 2) % 4, i).astype(BF16)
             hops.append(
@@ -475,6 +480,11 @@
         stage.append(reduce_to(send_two.at[1, d - 1], recv_two.at[1, d - 1], 15 + d, device(to, y, z, b)))
     own[0, 0:128, :] = summed(0, y)
     own[1, 0:128, :] = summed(1, x)
+    for n in range(WIDTH // 128):
+        at = slice(n * 128, (n + 1) * 128)
+        for u in range(2):
+            there = slice(u * 128, (u + 1) * 128)
+            out_gate_grad[there, at] = (grad_y[there, at].astype(F32) * conv_at(n, u)).astype(BF16)
     for copy in stage:
         copy.wait_recv()
     for h in range(2):
@@ -562,8 +572,8 @@
             DMA((33,)),
             DMA((26,)),
             DMA((26,)),
-            DMA((21,)),
-            DMA((21,)),
+            DMA((22,)),
+            DMA((22,)),
             DMA((OPERANDS,)),
         ]
         + [pltpu.VMEM(a.shape, a.dtype) for a in operands],

time: 119 us -> 120 us (level)
  no operation moved by 1% of the time
where the time goes in v5:
time: 120 us; the launch traced here: 119 us
  Pallas kernels  119 us (99%)
    pallas_call x1, Pallas kernels, on_device(): pl.pallas_call(kernel, name='hyena_backward', out_shape=outs, in_specs=[p...  115 us
    pallas_call x1, Pallas kernels, on_device(): pl.pallas_call(last_products, name='last_products', grid=(WIDTH // 256,),...  4.17 us

profile of v5, /device:TPU:64, one launch (start us, length us, event | category | flops | bytes accessed | tf_op | source)
XLA Modules:
  0.0 119.5 jit_solution(15575163076085680883)
XLA Ops:
  0.6 114.5 %hyena_backward.1 = (bf16[256,1024]{1,0:T(8,128)(2,1)}, bf16[64,2,16,256]{3,2,1,0:T(8,128)(2,1)}, f32[64,1024]{1,0:T(8,128)}) custom-call(bf16[256,1024]{1,0:T(8,128)(2,1)} %in_gate.1, bf16[256,1024]{1,0:T(8,128)(2,1)} %values.1, bf16[256,1024]{1,0:T(8,128)(2,1)} %refs_2_.1, bf16[64,1024]{1,0:T(8,128)(2,1)} %bitcast.2, bf16[256,4096]{1,0:T(8,128)(2,1)} %refs_4_.1, ...), custom_call_target="tpu_custom_call" | custom-call | tf_op jit(solution)/shard_map/hyena_backward/pallas_call | solution.py:537
  115.2 4.2 %last_products.1 = (bf16[256,1024]{1,0:T(8,128)(2,1)}, bf16[256,1024]{1,0:T(8,128)(2,1)}, bf16[256,1024]{1,0:T(8,128)(2,1)}, f32[256,1024]{1,0:T(8,128)}, f32[64,1024]{1,0:T(8,128)}) custom-call(bf16[64,2,16,256]{3,2,1,0:T(8,128)(2,1)} %get-tuple-element.13.blocks, bf16[256,1024]{1,0:T(8,128)(2,1)} %in_gate.1, bf16[256,1024]{1,0:T(8,128)(2,1)} %values.1, ...), custom_call_target="tpu_custom_call" | custom-call | tf_op jit(solution)/shard_map/last_products/pallas_call | solution.py:585
